TPU v7x, 128 devices: a whole 4x4x4 slice. The times are simulated.
128 devices in a mesh: ctx: 8 (over x_hi, z), head: 4 (over y), ret: 4 (over x_lo, core).
Axes of the slice: x: 4 (x_hi: 2, x_lo: 2; x = x_hi * 2 + x_lo), y: 4, z: 4, core: 2. Of those that a mesh axis runs over, the one named last changes fastest.
Arguments:
- self_query: bfloat16 [4, 1024, 4096], P('ret', 'ctx', 'head'), may hold values from -2.5 to 2.5
- self_key: bfloat16 [4, 1024, 4096], P('ret', 'ctx', 'head'), may hold values from -2.5 to 2.5
- self_value: bfloat16 [4, 1024, 4096], P('ret', 'ctx', 'head'), may hold values from -6 to 6
- self_grad: bfloat16 [4, 1024, 4096], P('ret', 'ctx', 'head'), may hold values from -192 to 192
- self_docs: int32 [4, 1024], P('ret', 'ctx'), may hold values from 0 to 3, never falling along the last dimension, each value on 1 to 512 neighbouring positions
- cross_query: bfloat16 [4, 1024, 4096], P('ret', 'ctx', 'head'), may hold values from -2.5 to 2.5
- cross_grad: bfloat16 [4, 1024, 4096], P('ret', 'ctx', 'head'), may hold values from -96 to 96
- neighbours: int32 [4, 16, 2], P('ret', 'ctx'), may hold values from 0 to 127, as said below
- encodings: bfloat16 [1024, 128, 512], P(('ctx', 'head', 'ret')), may hold values from -6 to 6
- key_weight: bfloat16 [512, 4096], P(None, 'head'), may hold values from -0.25 to 0.25
- value_weight: bfloat16 [512, 4096], P(None, 'head'), may hold values from -0.25 to 0.25
Outputs:
- query_grad: bfloat16 [4, 1024, 4096], P('ret', 'ctx', 'head')
- key_grad: bfloat16 [4, 1024, 4096], P('ret', 'ctx', 'head')
- value_grad: bfloat16 [4, 1024, 4096], P('ret', 'ctx', 'head')
- cross_query_grad: bfloat16 [4, 1024, 4096], P('ret', 'ctx', 'head')
- encoding_grad: bfloat16 [1024, 128, 512], P(('ctx', 'head', 'ret'))
Inputs may be any that keep to these rules, and one draw needn't show every extreme that they name: `self_docs`: document numbers never fall along a sequence; each document has 1 to 512 tokens. `neighbours`: an entry v of a span in context block g names pool row g * 16 * 8 + v, held by owner v // 8 of that block (owners counted over head, then ret). Among the 4 entries of one sequence's context block, at most 2 name the same owner. The 2 entries of a span differ.
All inputs are finite; a program needn't handle non-finite values.
Results may differ from a plain program's by a relative error of at most 0.0073.
Values may be sent and summed in bfloat16 or wider, within the bound.
A program may use at most 128 MiB of HBM per device.

v0:
```python
import functools
import math

import jax
import jax.numpy as jnp
from jax import lax
from jax.experimental import pallas as pl
from jax.experimental.pallas import tpu as pltpu
from jax.sharding import PartitionSpec as P

SPAN = 64
NBR = 2
NR = 128
E = 512
DH = 128
POOL_DEV = 8
EPSILON = 1e-06
SCALE = 1.0 / math.sqrt(DH)

N_CTX = 8
N_HEAD = 4
N_RET = 4
ENTRIES = 4
BLOCK = 128
TILE = 256
QUARTER = E // N_HEAD
CHUNKS = 2
CHUNK = NR // CHUNKS
FINAL = 2
FINAL_ROWS = NR // FINAL

MESH = pl.DeviceIdType.MESH
F32 = jnp.float32
BF16 = jnp.bfloat16


def dot(a, b):
    return lax.dot_general(a, b, (((1,), (0,)), ((), ())), preferred_element_type=F32)


def dot_nt(a, b):
    return lax.dot_general(a, b, (((1,), (1,)), ((), ())), preferred_element_type=F32)


def kernel(
    sq, sk, sv, sg, docs, cq, cg, nbr, enc, wk, wv,
    oq, ok, ov, ocq, oenc,
    lists_v, lists_s, docs_v, doc_cols, pool, outgoing, incoming, rows, held, key_acc, value_acc, grads,
    wk_v, wv_v, cq_v, cg_v, cross_out, partial, parts_out, parts_in, shares, owned,
    loc, s_list, r_list, s_docs, r_docs, s_pool, r_pool, s_ret, r_ret, s_rows, r_rows, s_self, r_self,
    s_part, r_part, s_share, r_share, s_own, r_own, s_back, r_back,
):
    c, h, r = lax.axis_index("ctx"), lax.axis_index("head"), lax.axis_index("ret")

    def over_ctx(d):
        return lax.rem(c + d, N_CTX)

    def over_head(d):
        return lax.rem(h + d, N_HEAD)

    def over_ret(d):
        return lax.rem(r + d, N_RET)

    def send(src, dst, ssem, rsem, device):
        copy = pltpu.make_async_remote_copy(
            src_ref=src, dst_ref=dst, send_sem=ssem, recv_sem=rsem,
            device_id=device, device_id_type=MESH,
        )
        copy.start()
        return copy

    local_count = [0]

    def keep(src, dst):
        copy = pltpu.make_async_copy(src, dst, loc.at[local_count[0]])
        local_count[0] += 1
        copy.start()
        return copy

    sent = []

    lane = lax.broadcasted_iota(jnp.int32, (8, 128), 1)
    tile = jnp.zeros((8, 128), jnp.int32)
    for e in range(ENTRIES):
        tile = jnp.where(lane == e, nbr[0, e // NBR, e % NBR], tile)
    lists_v[r] = tile

    barrier = pltpu.get_barrier_semaphore()
    peers = [(over_ctx(d), h, r) for d in range(1, N_CTX)]
    peers += [(c, over_head(d), r) for d in range(1, N_HEAD)]
    peers += [(c, h, over_ret(d)) for d in range(1, N_RET)]
    for peer in peers:
        pl.semaphore_signal(barrier, inc=1, device_id=peer, device_id_type=MESH)
    pl.semaphore_wait(barrier, len(peers))

    list_copies = [
        send(lists_v.at[r], lists_v.at[r], s_list.at[d - 1], r_list.at[d - 1], (c, h, over_ret(d)))
        for d in range(1, N_RET)
    ]

    def quarter_of(owner_column, t):
        return enc.at[:, pl.ds(t * CHUNK, CHUNK), pl.ds(pl.multiple_of(owner_column * QUARTER, 128), QUARTER)]

    pool_copies = []
    pool_own = []
    for t in range(CHUNKS):
        pool_copies.append([
            send(
                quarter_of(over_head(d), t),
                pool[t].at[pl.ds(h * POOL_DEV, POOL_DEV)],
                s_pool.at[t * 3 + d - 1], r_pool.at[t * 3 + d - 1], (c, over_head(d), r),
            )
            for d in (2, 1, 3)
        ])
        pool_own.append(
            keep(quarter_of(h, t), pool[t].at[pl.ds(h * POOL_DEV, POOL_DEV)])
        )
    doc_copies = [
        send(docs, docs_v.at[c], s_docs.at[d - 1], r_docs.at[d - 1], (over_ctx(d), h, r))
        for d in range(1, N_CTX)
    ]
    doc_own = keep(docs, docs_v.at[c])
    self_in = (sq, sk, sv, sg)

    def head_of(array, number):
        return array.at[0, :, pl.ds(pl.multiple_of(number * DH, 128), DH)]

    self_copies = []
    for d in (6, 2, 5, 3, 7, 1, 4):
        for a in range(4):
            at = (d - 1) * 4 + a
            self_copies.append(send(
                head_of(self_in[a], over_ctx(d)),
                held.at[a, pl.ds(pl.multiple_of(c * BLOCK, 128), BLOCK)],
                s_self.at[at], r_self.at[at], (over_ctx(d), h, r),
            ))
    self_own = [
        keep(head_of(self_in[a], c), held.at[a, pl.ds(pl.multiple_of(c * BLOCK, 128), BLOCK)])
        for a in range(4)
    ]
    cross_own = [keep(wk, wk_v), keep(wv, wv_v), keep(cq.at[0], cq_v), keep(cg.at[0], cg_v)]

    for copy in list_copies:
        copy.wait_recv()
    sent.extend(list_copies)
    to_scalars = keep(lists_v, lists_s)
    to_scalars.wait()

    ret_copies = []
    for t in range(CHUNKS):
        here = pl.ds(t * CHUNK, CHUNK)
        pool_own[t].wait()
        for copy in pool_copies[t]:
            copy.wait_recv()
        sent.extend(pool_copies[t])
        for q in range(N_RET):
            for e in range(ENTRIES):
                value = lists_s[q, 0, e]
                place = lax.div(value, N_RET * POOL_DEV) * POOL_DEV + lax.rem(value, POOL_DEV)
                outgoing[q * ENTRIES + e, here] = pool[t][place]
        own = [
            keep(
                outgoing.at[pl.ds(r * ENTRIES, ENTRIES), here],
                incoming[t].at[pl.ds(r * ENTRIES, ENTRIES)],
            )
        ]
        ret_copies.append((own, [
            send(
                outgoing.at[pl.ds(over_ret(d) * ENTRIES, ENTRIES), here],
                incoming[t].at[pl.ds(r * ENTRIES, ENTRIES)],
                s_ret.at[t * 3 + d - 1], r_ret.at[t * 3 + d - 1], (c, h, over_ret(d)),
            )
            for d in (2, 1, 3)
        ]))

    row_copies = []
    my_columns = pl.ds(pl.multiple_of(h * QUARTER, 128), QUARTER)
    for t in range(CHUNKS):
        here = pl.ds(t * CHUNK, CHUNK)
        own, copies = ret_copies[t]
        for copy in own:
            copy.wait()
        for copy in copies:
            copy.wait_recv()
        sent.extend(copies)
        for e in range(ENTRIES):
            value = lists_s[r, 0, e]
            column = lax.rem(lax.div(value, POOL_DEV), N_RET)
            rows[e, here, my_columns] = incoming[t][column * ENTRIES + e]
        row_copies.append([
            send(
                rows.at[:, here, my_columns], rows.at[:, here, my_columns],
                s_rows.at[t * 3 + d - 1], r_rows.at[t * 3 + d - 1], (c, over_head(d), r),
            )
            for d in (2, 1, 3)
        ])

    for copy in cross_own:
        copy.wait()
    for copies in row_copies:
        for copy in copies:
            copy.wait_recv()
        sent.extend(copies)

    lanes = lax.broadcasted_iota(jnp.int32, (SPAN, TILE), 1)

    def paired(block):
        low = jnp.where(lanes < DH, block, jnp.zeros_like(block))
        high = jnp.where(lanes >= DH, block, jnp.zeros_like(block))
        return jnp.concatenate([low, high], axis=0)

    def cross_span(s):
        tokens = rows[s * NBR:(s + 1) * NBR].reshape(NBR * NR, E)
        here = slice(s * SPAN, (s + 1) * SPAN)
        for p in range(4):
            cols = slice(p * TILE, (p + 1) * TILE)
            keys_raw = dot(tokens, wk_v[:, cols])
            values_b = dot(tokens, wv_v[:, cols]).astype(BF16)
            factors, normed = [], []
            for a in range(2):
                one = keys_raw[:, a * DH:(a + 1) * DH]
                factor = lax.rsqrt(jnp.sum(one * one, axis=1, keepdims=True) * (1.0 / DH) + EPSILON)
                factors.append(factor)
                normed.append(one * factor)
            keys_b = jnp.concatenate([n.astype(BF16) for n in normed], axis=1)
            query = paired(cq_v[here, cols])
            grad = paired(cg_v[here, cols])
            raw = jnp.exp(dot_nt(keys_b, query) * SCALE)
            probs = raw * (1.0 / jnp.sum(raw, axis=0, keepdims=True))
            probs_b = probs.astype(BF16)
            dprobs = dot_nt(values_b, grad)
            cdeltas = jnp.sum(probs_b.astype(F32) * dprobs, axis=0, keepdims=True)
            dscores = probs * (dprobs - cdeltas)
            dscores_b = dscores.astype(BF16)
            query_part = dot(dscores.T.astype(BF16), keys_b) * SCALE
            cross_out[here, p * TILE:p * TILE + DH] = query_part[:SPAN, :DH].astype(BF16)
            cross_out[here, p * TILE + DH:(p + 1) * TILE] = query_part[SPAN:, DH:].astype(BF16)
            grad_keys = dot(dscores_b, query) * SCALE
            grad_values = dot(probs_b, grad).astype(BF16)
            raws = []
            for a in range(2):
                one = grad_keys[:, a * DH:(a + 1) * DH]
                mean = jnp.sum(normed[a] * one, axis=1, keepdims=True) * (1.0 / DH)
                raws.append((factors[a] * (one - normed[a] * mean)).astype(BF16))
            grad_raw = jnp.concatenate(raws, axis=1)
            term = dot_nt(grad_raw, wk_v[:, cols]) + dot_nt(grad_values, wv_v[:, cols])
            if p == 0:
                partial[...] = term
            else:
                partial[...] += term
        for q in range(N_HEAD):
            parts_out[q, s * NBR * NR:(s + 1) * NBR * NR] = partial[:, q * QUARTER:(q + 1) * QUARTER].astype(BF16)
        span_rows = pl.ds(s * NBR * NR, NBR * NR)
        return [
            send(
                parts_out.at[over_head(d), span_rows], parts_in.at[h, span_rows],
                s_part.at[s * 3 + d - 1], r_part.at[s * 3 + d - 1], (c, over_head(d), r),
            )
            for d in (2, 1, 3)
        ]

    part_copies = [cross_span(s) for s in range(2)]
    cross_done = keep(cross_out, ocq.at[0])

    def share_span(s):
        span_rows = slice(s * NBR * NR, (s + 1) * NBR * NR)
        for copy in part_copies[s]:
            copy.wait_recv()
        sent.extend(part_copies[s])
        total = parts_out[h, span_rows].astype(F32)
        for d in range(1, N_HEAD):
            total = total + parts_in[over_head(d), span_rows].astype(F32)
        mine = pl.ds(r * ENTRIES + s * NBR, NBR)
        shares[mine] = total.astype(BF16).reshape(NBR, NR, QUARTER)
        return [
            send(
                shares.at[mine], shares.at[mine],
                s_share.at[s * 3 + d - 1], r_share.at[s * 3 + d - 1], (c, h, over_ret(d)),
            )
            for d in (2, 1, 3)
        ]

    def prepare_self():
        doc_own.wait()
        for copy in doc_copies + self_copies:
            copy.wait_recv()
        for copy in self_own:
            copy.wait()
        sent.extend(doc_copies + self_copies)
        for b in range(N_CTX):
            one = jnp.broadcast_to(docs_v[b].astype(F32), (BLOCK, BLOCK))
            doc_cols[b * BLOCK:(b + 1) * BLOCK] = one.T

    key_at = lax.broadcasted_iota(jnp.int32, (TILE, TILE), 0)
    query_at = lax.broadcasted_iota(jnp.int32, (TILE, TILE), 1)

    def self_rows(i):
        mine = slice(i * TILE, (i + 1) * TILE)
        query, grad = held[0, mine], held[3, mine]
        query_docs = jnp.concatenate([docs_v[2 * i], docs_v[2 * i + 1]], axis=1).astype(F32)
        first = max(0, i - 2)
        totals = jnp.zeros((1, TILE), F32)
        deltas = jnp.zeros((1, TILE), F32)
        raws, dnormeds = [], []
        for j in range(first, i + 1):
            there = slice(j * TILE, (j + 1) * TILE)
            key_docs = doc_cols[there]
            visible = jnp.concatenate([key_docs, key_docs], axis=1) == query_docs
            if j == i:
                visible = visible & (key_at <= query_at)
            raw = jnp.where(visible, jnp.exp(dot_nt(held[1, there], query) * SCALE), 0.0)
            dnormed = dot_nt(held[2, there], grad)
            totals = totals + jnp.sum(raw, axis=0, keepdims=True)
            deltas = deltas + jnp.sum(raw.astype(BF16).astype(F32) * dnormed, axis=0, keepdims=True)
            raws.append(raw)
            dnormeds.append(dnormed)
        inverse = 1.0 / totals
        deltas = deltas * inverse
        query_sum = jnp.zeros((DH, TILE), F32)
        for j in range(first, i + 1):
            there = slice(j * TILE, (j + 1) * TILE)
            normed = raws[j - first] * inverse
            dscores = (normed * (dnormeds[j - first] - deltas)).astype(BF16)
            query_sum = query_sum + dot(held[1, there].astype(F32).T.astype(BF16), dscores)
            key_term = dot(dscores, query)
            value_term = dot(normed.astype(BF16), grad)
            if j == i:
                key_acc[there] = key_term
                value_acc[there] = value_term
            else:
                key_acc[there] += key_term
                value_acc[there] += value_term
        grads[0, mine] = (query_sum * SCALE).T.astype(BF16)

    def self_back():
        outs = (oq, ok, ov)
        copies = []
        for d in (6, 2, 5, 3, 7, 1, 4):
            for a in range(3):
                at = (d - 1) * 3 + a
                copies.append(send(
                    grads.at[a, pl.ds(pl.multiple_of(over_ctx(d) * BLOCK, 128), BLOCK)],
                    head_of(outs[a], c),
                    s_back.at[at], r_back.at[at], (over_ctx(d), h, r),
                ))
        own = [
            keep(grads.at[a, pl.ds(pl.multiple_of(c * BLOCK, 128), BLOCK)], head_of(outs[a], c))
            for a in range(3)
        ]
        return copies, own

    prepare_self()
    self_rows(0)
    share_copies = [share_span(0)]
    self_rows(1)
    share_copies.append(share_span(1))
    self_rows(2)
    self_rows(3)
    grads[1] = (key_acc[...] * SCALE).astype(BF16)
    grads[2] = value_acc[...].astype(BF16)
    back_copies, back_own = self_back()

    for copies in share_copies:
        for copy in copies:
            copy.wait_recv()
        sent.extend(copies)

    GROUP = 16
    lane_e = lax.broadcasted_iota(jnp.int32, (1, N_RET * ENTRIES * GROUP), 1)
    named = jnp.zeros((1, N_RET * ENTRIES * GROUP), jnp.int32)
    for q in range(N_RET):
        for e in range(ENTRIES):
            k = q * ENTRIES + e
            named = jnp.where(lane_e // GROUP == k, lists_s[q, 0, e], named)
    wide = (N_HEAD * POOL_DEV * GROUP, N_RET * ENTRIES * GROUP)
    target = lax.broadcasted_iota(jnp.int32, wide, 0)
    slot = target // GROUP
    wanted = ((slot // POOL_DEV) * N_RET + r) * POOL_DEV + slot % POOL_DEV
    same_token = target % GROUP == lax.broadcasted_iota(jnp.int32, wide, 1) % GROUP
    selector = jnp.where((wanted == named) & same_token, 1.0, 0.0).astype(BF16)

    own_copies = []
    own_kept = []
    for f in range(FINAL):
        for t in range(FINAL_ROWS // GROUP):
            at = slice(f * FINAL_ROWS + t * GROUP, f * FINAL_ROWS + (t + 1) * GROUP)
            stacked = shares[:, at].reshape(N_RET * ENTRIES * GROUP, QUARTER)
            summed = dot(selector, stacked)
            owned[:, at] = summed.astype(BF16).reshape(N_HEAD * POOL_DEV, GROUP, QUARTER)
        here = pl.ds(f * FINAL_ROWS, FINAL_ROWS)
        for d in (2, 1, 3):
            own_copies.append(send(
                owned.at[pl.ds(over_head(d) * POOL_DEV, POOL_DEV), here], oenc.at[:, here, my_columns],
                s_own.at[f * 3 + d - 1], r_own.at[f * 3 + d - 1], (c, over_head(d), r),
            ))
        own_kept.append(keep(owned.at[pl.ds(h * POOL_DEV, POOL_DEV), here], oenc.at[:, here, my_columns]))

    cross_done.wait()
    for copy in back_own + own_kept:
        copy.wait()
    for copy in back_copies + own_copies:
        copy.wait_recv()
    sent.extend(back_copies + own_copies)
    for copy in sent:
        copy.wait_send()


def on_device(
    self_query, self_key, self_value, self_grad, self_docs, cross_query, cross_grad,
    neighbours, encodings, key_weight, value_weight,
):
    block = jax.ShapeDtypeStruct(self_query.shape, BF16)
    any_space = pl.BlockSpec(memory_space=pltpu.HBM)
    in_specs = [any_space] * 11
    in_specs[7] = pl.BlockSpec(memory_space=pltpu.SMEM)
    dma = pltpu.SemaphoreType.DMA
    scratch = [
        pltpu.VMEM((N_RET, 8, 128), jnp.int32),
        pltpu.SMEM((N_RET, 8, 128), jnp.int32),
        pltpu.VMEM((N_CTX, 1, BLOCK), jnp.int32),
        pltpu.VMEM((N_CTX * BLOCK, 128), F32),
        (pltpu.VMEM((N_HEAD * POOL_DEV, CHUNK, QUARTER), BF16),) * CHUNKS,
        pltpu.VMEM((N_RET * ENTRIES, NR, QUARTER), BF16),
        (pltpu.VMEM((N_RET * ENTRIES, CHUNK, QUARTER), BF16),) * CHUNKS,
        pltpu.VMEM((ENTRIES, NR, E), BF16),
        pltpu.VMEM((4, N_CTX * BLOCK, DH), BF16),
        pltpu.VMEM((N_CTX * BLOCK, DH), F32),
        pltpu.VMEM((N_CTX * BLOCK, DH), F32),
        pltpu.VMEM((3, N_CTX * BLOCK, DH), BF16),
        pltpu.VMEM(key_weight.shape, BF16),
        pltpu.VMEM(value_weight.shape, BF16),
        pltpu.VMEM(cross_query.shape[1:], BF16),
        pltpu.VMEM(cross_grad.shape[1:], BF16),
        pltpu.VMEM(cross_grad.shape[1:], BF16),
        pltpu.VMEM((NBR * NR, E), F32),
        pltpu.VMEM((N_HEAD, ENTRIES * NR, QUARTER), BF16),
        pltpu.VMEM((N_HEAD, ENTRIES * NR, QUARTER), BF16),
        pltpu.VMEM((N_RET * ENTRIES, NR, QUARTER), BF16),
        pltpu.VMEM((N_HEAD * POOL_DEV, NR, QUARTER), BF16),
        dma((24,)),
        dma((3,)), dma((3,)),
        dma((7,)), dma((7,)),
        dma((3 * CHUNKS,)), dma((3 * CHUNKS,)),
        dma((3 * CHUNKS,)), dma((3 * CHUNKS,)),
        dma((3 * CHUNKS,)), dma((3 * CHUNKS,)),
        dma((28,)), dma((28,)),
        dma((6,)), dma((6,)),
        dma((6,)), dma((6,)),
        dma((3 * FINAL,)), dma((3 * FINAL,)),
        dma((21,)), dma((21,)),
    ]
    return pl.pallas_call(
        kernel,
        out_shape=(block, block, block, block, jax.ShapeDtypeStruct(encodings.shape, BF16)),
        in_specs=in_specs,
        out_specs=(any_space,) * 5,
        scratch_shapes=scratch,
        compiler_params=pltpu.CompilerParams(
            collective_id=0, has_side_effects=True, vmem_limit_bytes=64 * 2**20
        ),
        name="retro_backward",
    )(
        self_query, self_key, self_value, self_grad, self_docs, cross_query, cross_grad,
        neighbours, encodings, key_weight, value_weight,
    )


def solution(mesh):
    tokens = P("ret", "ctx", "head")
    pool = P(("ctx", "head", "ret"), None, None)
    placed = (
        tokens, tokens, tokens, tokens, P("ret", "ctx"), tokens, tokens,
        P("ret", "ctx", None), pool, P(None, "head"), P(None, "head"),
    )
    return jax.shard_map(
        on_device,
        mesh=mesh,
        in_specs=placed,
        out_specs=(tokens, tokens, tokens, tokens, pool),
        check_vma=False,
    )
```

profile of v0, /device:TPU:0, one launch (start us, length us, event | category | flops | bytes accessed | tf_op | source)
XLA Modules:
  0.0 72.7 jit_solution(10891597433269857140)
XLA Ops:
  0.6 66.2 %retro_backward.1 = (bf16[1,128,1024]{2,1,0:T(8,128)(2,1)}, bf16[1,128,1024]{2,1,0:T(8,128)(2,1)}, bf16[1,128,1024]{2,1,0:T(8,128)(2,1)}, bf16[1,128,1024]{2,1,0:T(8,128)(2,1)}, bf16[8,128,512]{2,1,0:T(8,128)(2,1)}) custom-call(bf16[1,128,1024]{2,1,0:T(8,128)(2,1)} %sq.1, bf16[1,128,1024]{2,1,0:T(8,128)(2,1)} %sk.1, bf16[1,128,1024]{2,1,0:T(8,128)(2,1)} %sv.1, ...), custom_call_target="tpu_custom_call" | custom-call | tf_op jit(solution)/shard_map/retro_backward/pallas_call | solution.py:452
  66.8 0.0 copy-start.2
  66.8 0.0 copy-start
  66.8 1.8 %copy.21 = bf16[1,128,1024]{2,1,0:T(8,128)(2,1)} copy(bf16[1,128,1024]{2,1,0:T(8,128)(2,1)} %get-tuple-element.10) | data formatting | bytes 524288
  68.6 0.0 copy-done.2
  68.6 0.7 copy.22
  69.3 0.0 copy-start.1
  69.3 1.7 %copy.23 = bf16[1,128,1024]{2,1,0:T(8,128)(2,1)} copy(bf16[1,128,1024]{2,1,0:T(8,128)(2,1)} %get-tuple-element.12) | data formatting | bytes 524288
  71.0 0.0 copy-done.1
  71.0 0.7 copy.24
  71.7 0.0 copy-done
  71.7 1.0 %copy.25 = bf16[8,128,512]{2,1,0:T(8,128)(2,1)} copy(bf16[8,128,512]{2,1,0:T(8,128)(2,1)S(1)} %copy-done) | data formatting | bytes 2097152
Async XLA Ops:
  66.8 1.8 %copy-start.2 = (bf16[1,128,1024]{2,1,0:T(8,128)(2,1)S(1)}, bf16[1,128,1024]{2,1,0:T(8,128)(2,1)}, u32[]{:S(2)}) copy-start(bf16[1,128,1024]{2,1,0:T(8,128)(2,1)} %get-tuple-element.11) | copy-start | bytes 786436
  66.8 4.9 %copy-start = (bf16[8,128,512]{2,1,0:T(8,128)(2,1)S(1)}, bf16[8,128,512]{2,1,0:T(8,128)(2,1)}, u32[]{:S(2)}) copy-start(bf16[8,128,512]{2,1,0:T(8,128)(2,1)} %get-tuple-element.14) | copy-start | bytes 3145732
  69.3 1.7 %copy-start.1 = (bf16[1,128,1024]{2,1,0:T(8,128)(2,1)S(1)}, bf16[1,128,1024]{2,1,0:T(8,128)(2,1)}, u32[]{:S(2)}) copy-start(bf16[1,128,1024]{2,1,0:T(8,128)(2,1)} %get-tuple-element.13) | copy-start | bytes 786436
where the time goes:
time: 73.9 us; the launch traced here: 72.7 us
  Pallas kernels  66.2 us (90%)
  local copies, waits for them, and re-layouts  5.87 us (8%)
    pallas_call x1, Pallas kernels, on_device(): pl.pallas_call(kernel, out_shape=(block, block, block, block, jax.ShapeDt...  66.2 us
    unnamed x11, local copies, waits for them, and re-layouts  5.87 us

commit v1 on v0

--- a/solution.py
+++ b/solution.py
@@ -26,8 +26,6 @@
 QUARTER = E // N_HEAD
 CHUNKS = 2
 CHUNK = NR // CHUNKS
-FINAL = 2
-FINAL_ROWS = NR // FINAL
 
 MESH = pl.DeviceIdType.MESH
 F32 = jnp.float32
@@ -46,7 +44,7 @@
     sq, sk, sv, sg, docs, cq, cg, nbr, enc, wk, wv,
     oq, ok, ov, ocq, oenc,
     lists_v, lists_s, docs_v, doc_cols, pool, outgoing, incoming, rows, held, key_acc, value_acc, grads,
-    wk_v, wv_v, cq_v, cg_v, cross_out, partial, parts_out, parts_in, shares, owned,
+    wk_v, wv_v, cq_v, cg_v, cross_out, keys_n, factors, keys_b, values_b, raw_grads, value_grads, parts_out, parts_in, shares, owned,
     loc, s_list, r_list, s_docs, r_docs, s_pool, r_pool, s_ret, r_ret, s_rows, r_rows, s_self, r_self,
     s_part, r_part, s_share, r_share, s_own, r_own, s_back, r_back,
 ):
@@ -67,8 +65,10 @@
             device_id=device, device_id_type=MESH,
         )
         copy.start()
+        every.append(copy)
         return copy
 
+    every = []
     local_count = [0]
 
     def keep(src, dst):
@@ -76,8 +76,6 @@
         local_count[0] += 1
         copy.start()
         return copy
-
-    sent = []
 
     lane = lax.broadcasted_iota(jnp.int32, (8, 128), 1)
     tile = jnp.zeros((8, 128), jnp.int32)
@@ -126,23 +124,27 @@
         return array.at[0, :, pl.ds(pl.multiple_of(number * DH, 128), DH)]
 
     self_copies = []
-    for d in (6, 2, 5, 3, 7, 1, 4):
+    self_own = []
+
+    def self_start():
+        for d in (6, 2, 5, 3, 7, 1, 4):
+            for a in range(4):
+                at = (d - 1) * 4 + a
+                self_copies.append(send(
+                    head_of(self_in[a], over_ctx(d)),
+                    held.at[a, pl.ds(pl.multiple_of(c * BLOCK, 128), BLOCK)],
+                    s_self.at[at], r_self.at[at], (over_ctx(d), h, r),
+                ))
         for a in range(4):
-            at = (d - 1) * 4 + a
-            self_copies.append(send(
-                head_of(self_in[a], over_ctx(d)),
-                held.at[a, pl.ds(pl.multiple_of(c * BLOCK, 128), BLOCK)],
-                s_self.at[at], r_self.at[at], (over_ctx(d), h, r),
-            ))
-    self_own = [
-        keep(head_of(self_in[a], c), held.at[a, pl.ds(pl.multiple_of(c * BLOCK, 128), BLOCK)])
-        for a in range(4)
-    ]
+            self_own.append(
+                keep(head_of(self_in[a], c), held.at[a, pl.ds(pl.multiple_of(c * BLOCK, 128), BLOCK)])
+            )
+
+    self_start()
     cross_own = [keep(wk, wk_v), keep(wv, wv_v), keep(cq.at[0], cq_v), keep(cg.at[0], cg_v)]
 
     for copy in list_copies:
         copy.wait_recv()
-    sent.extend(list_copies)
     to_scalars = keep(lists_v, lists_s)
     to_scalars.wait()
 
@@ -152,7 +154,6 @@
         pool_own[t].wait()
         for copy in pool_copies[t]:
             copy.wait_recv()
-        sent.extend(pool_copies[t])
         for q in range(N_RET):
             for e in range(ENTRIES):
                 value = lists_s[q, 0, e]
@@ -182,7 +183,6 @@
             copy.wait()
         for copy in copies:
             copy.wait_recv()
-        sent.extend(copies)
         for e in range(ENTRIES):
             value = lists_s[r, 0, e]
             column = lax.rem(lax.div(value, POOL_DEV), N_RET)
@@ -197,10 +197,30 @@
 
     for copy in cross_own:
         copy.wait()
-    for copies in row_copies:
-        for copy in copies:
+
+    def pieces(width):
+        return [slice(n * width, (n + 1) * width) for n in range(keys_b.shape[2] // width)]
+
+    def project(t):
+        here = slice(t * CHUNK, (t + 1) * CHUNK)
+        for copy in row_copies[t]:
             copy.wait_recv()
-        sent.extend(copies)
+        tokens = rows[:, here, :].reshape(ENTRIES * CHUNK, E)
+        for cols in pieces(TILE):
+            keys_raw = dot(tokens, wk_v[:, cols])
+            values_b[:, here, cols] = dot(tokens, wv_v[:, cols]).astype(BF16).reshape(ENTRIES, CHUNK, TILE)
+            for a in range(2):
+                one = keys_raw[:, a * DH:(a + 1) * DH]
+                mean = jnp.sum(one * one, axis=1, keepdims=True) * (1.0 / DH)
+                factor = jnp.broadcast_to(lax.rsqrt(mean + EPSILON), one.shape)
+                normed = one * factor
+                at = slice(cols.start + a * DH, cols.start + (a + 1) * DH)
+                factors[:, here, at] = factor.reshape(ENTRIES, CHUNK, DH)
+                keys_n[:, here, at] = normed.reshape(ENTRIES, CHUNK, DH)
+                keys_b[:, here, at] = normed.astype(BF16).reshape(ENTRIES, CHUNK, DH)
+
+    for t in range(CHUNKS):
+        project(t)
 
     lanes = lax.broadcasted_iota(jnp.int32, (SPAN, TILE), 1)
 
@@ -209,73 +229,74 @@
         high = jnp.where(lanes >= DH, block, jnp.zeros_like(block))
         return jnp.concatenate([low, high], axis=0)
 
-    def cross_span(s):
-        tokens = rows[s * NBR:(s + 1) * NBR].reshape(NBR * NR, E)
+    def attend(s):
         here = slice(s * SPAN, (s + 1) * SPAN)
-        for p in range(4):
-            cols = slice(p * TILE, (p + 1) * TILE)
-            keys_raw = dot(tokens, wk_v[:, cols])
-            values_b = dot(tokens, wv_v[:, cols]).astype(BF16)
-            factors, normed = [], []
+        mine = slice(s * NBR, (s + 1) * NBR)
+        pairs = pieces(TILE)
+
+        def span_of(array, cols):
+            return array[mine, :, cols].reshape(NBR * NR, cols.stop - cols.start)
+
+        queries = [paired(cq_v[here, cols]) for cols in pairs]
+        outer = [paired(cg_v[here, cols]) for cols in pairs]
+        raws = [jnp.exp(dot_nt(span_of(keys_b, cols), q) * SCALE) for cols, q in zip(pairs, queries)]
+        dprobs = [dot_nt(span_of(values_b, cols), g) for cols, g in zip(pairs, outer)]
+        probs = [raw * (1.0 / jnp.sum(raw, axis=0, keepdims=True)) for raw in raws]
+        probs_b = [p.astype(BF16) for p in probs]
+        cdeltas = [jnp.sum(p.astype(F32) * d, axis=0, keepdims=True) for p, d in zip(probs_b, dprobs)]
+        dscores = [p * (d - c) for p, d, c in zip(probs, dprobs, cdeltas)]
+        dscores_b = [d.astype(BF16) for d in dscores]
+        grad_keys = [dot(d, q) * SCALE for d, q in zip(dscores_b, queries)]
+        for cols, p, g in zip(pairs, probs_b, outer):
+            value_grads[mine, :, cols] = dot(p, g).astype(BF16).reshape(NBR, NR, TILE)
+        for cols, d in zip(pairs, dscores):
+            part = dot(d.T.astype(BF16), span_of(keys_b, cols)) * SCALE
+            cross_out[here, cols.start:cols.start + DH] = part[:SPAN, :DH].astype(BF16)
+            cross_out[here, cols.start + DH:cols.stop] = part[SPAN:, DH:].astype(BF16)
+        for cols, grad in zip(pairs, grad_keys):
             for a in range(2):
-                one = keys_raw[:, a * DH:(a + 1) * DH]
-                factor = lax.rsqrt(jnp.sum(one * one, axis=1, keepdims=True) * (1.0 / DH) + EPSILON)
-                factors.append(factor)
-                normed.append(one * factor)
-            keys_b = jnp.concatenate([n.astype(BF16) for n in normed], axis=1)
-            query = paired(cq_v[here, cols])
-            grad = paired(cg_v[here, cols])
-            raw = jnp.exp(dot_nt(keys_b, query) * SCALE)
-            probs = raw * (1.0 / jnp.sum(raw, axis=0, keepdims=True))
-            probs_b = probs.astype(BF16)
-            dprobs = dot_nt(values_b, grad)
-            cdeltas = jnp.sum(probs_b.astype(F32) * dprobs, axis=0, keepdims=True)
-            dscores = probs * (dprobs - cdeltas)
-            dscores_b = dscores.astype(BF16)
-            query_part = dot(dscores.T.astype(BF16), keys_b) * SCALE
-            cross_out[here, p * TILE:p * TILE + DH] = query_part[:SPAN, :DH].astype(BF16)
-            cross_out[here, p * TILE + DH:(p + 1) * TILE] = query_part[SPAN:, DH:].astype(BF16)
-            grad_keys = dot(dscores_b, query) * SCALE
-            grad_values = dot(probs_b, grad).astype(BF16)
-            raws = []
-            for a in range(2):
-                one = grad_keys[:, a * DH:(a + 1) * DH]
-                mean = jnp.sum(normed[a] * one, axis=1, keepdims=True) * (1.0 / DH)
-                raws.append((factors[a] * (one - normed[a] * mean)).astype(BF16))
-            grad_raw = jnp.concatenate(raws, axis=1)
-            term = dot_nt(grad_raw, wk_v[:, cols]) + dot_nt(grad_values, wv_v[:, cols])
-            if p == 0:
-                partial[...] = term
-            else:
-                partial[...] += term
+                at = slice(cols.start + a * DH, cols.start + (a + 1) * DH)
+                one = grad[:, a * DH:(a + 1) * DH]
+                normed = span_of(keys_n, at)
+                mean = jnp.sum(normed * one, axis=1, keepdims=True) * (1.0 / DH)
+                raw = span_of(factors, at) * (one - normed * mean)
+                raw_grads[mine, :, at] = raw.astype(BF16).reshape(NBR, NR, DH)
+
+    for s in range(2):
+        attend(s)
+    cross_done = keep(cross_out, ocq.at[0])
+
+    def scatter(t):
+        here = pl.ds(t * CHUNK, CHUNK)
+        shape = (ENTRIES * CHUNK, keys_b.shape[2])
+        term = dot_nt(raw_grads[:, here, :].reshape(shape), wk_v[...])
+        term = term + dot_nt(value_grads[:, here, :].reshape(shape), wv_v[...])
         for q in range(N_HEAD):
-            parts_out[q, s * NBR * NR:(s + 1) * NBR * NR] = partial[:, q * QUARTER:(q + 1) * QUARTER].astype(BF16)
-        span_rows = pl.ds(s * NBR * NR, NBR * NR)
+            one = term[:, q * QUARTER:(q + 1) * QUARTER].astype(BF16)
+            parts_out[q, :, here, :] = one.reshape(ENTRIES, CHUNK, QUARTER)
         return [
             send(
-                parts_out.at[over_head(d), span_rows], parts_in.at[h, span_rows],
-                s_part.at[s * 3 + d - 1], r_part.at[s * 3 + d - 1], (c, over_head(d), r),
+                parts_out.at[over_head(d), :, here], parts_in.at[h, :, here],
+                s_part.at[t * 3 + d - 1], r_part.at[t * 3 + d - 1], (c, over_head(d), r),
             )
             for d in (2, 1, 3)
         ]
 
-    part_copies = [cross_span(s) for s in range(2)]
-    cross_done = keep(cross_out, ocq.at[0])
-
-    def share_span(s):
-        span_rows = slice(s * NBR * NR, (s + 1) * NBR * NR)
-        for copy in part_copies[s]:
+    part_copies = [scatter(t) for t in range(CHUNKS)]
+
+    def share(t):
+        here = pl.ds(t * CHUNK, CHUNK)
+        for copy in part_copies[t]:
             copy.wait_recv()
-        sent.extend(part_copies[s])
-        total = parts_out[h, span_rows].astype(F32)
+        total = parts_out[h, :, here, :].astype(F32)
         for d in range(1, N_HEAD):
-            total = total + parts_in[over_head(d), span_rows].astype(F32)
-        mine = pl.ds(r * ENTRIES + s * NBR, NBR)
-        shares[mine] = total.astype(BF16).reshape(NBR, NR, QUARTER)
+            total = total + parts_in[over_head(d), :, here, :].astype(F32)
+        mine = pl.ds(r * ENTRIES, ENTRIES)
+        shares[mine, here] = total.astype(BF16)
         return [
             send(
-                shares.at[mine], shares.at[mine],
-                s_share.at[s * 3 + d - 1], r_share.at[s * 3 + d - 1], (c, h, over_ret(d)),
+                shares.at[mine, here], shares.at[mine, here],
+                s_share.at[t * 3 + d - 1], r_share.at[t * 3 + d - 1], (c, h, over_ret(d)),
             )
             for d in (2, 1, 3)
         ]
@@ -286,7 +307,6 @@
             copy.wait_recv()
         for copy in self_own:
             copy.wait()
-        sent.extend(doc_copies + self_copies)
         for b in range(N_CTX):
             one = jnp.broadcast_to(docs_v[b].astype(F32), (BLOCK, BLOCK))
             doc_cols[b * BLOCK:(b + 1) * BLOCK] = one.T
@@ -332,6 +352,10 @@
                 value_acc[there] += value_term
         grads[0, mine] = (query_sum * SCALE).T.astype(BF16)
 
+    def self_finish():
+        grads[1] = (key_acc[...] * SCALE).astype(BF16)
+        grads[2] = value_acc[...].astype(BF16)
+
     def self_back():
         outs = (oq, ok, ov)
         copies = []
@@ -351,19 +375,14 @@
 
     prepare_self()
     self_rows(0)
-    share_copies = [share_span(0)]
     self_rows(1)
-    share_copies.append(share_span(1))
+    share_copies = [share(0)]
     self_rows(2)
+    share_copies.append(share(1))
     self_rows(3)
-    grads[1] = (key_acc[...] * SCALE).astype(BF16)
-    grads[2] = value_acc[...].astype(BF16)
+    self_finish()
+    back_copies, back_own = [], []
     back_copies, back_own = self_back()
-
-    for copies in share_copies:
-        for copy in copies:
-            copy.wait_recv()
-        sent.extend(copies)
 
     GROUP = 16
     lane_e = lax.broadcasted_iota(jnp.int32, (1, N_RET * ENTRIES * GROUP), 1)
@@ -381,17 +400,19 @@
 
     own_copies = []
     own_kept = []
-    for f in range(FINAL):
-        for t in range(FINAL_ROWS // GROUP):
-            at = slice(f * FINAL_ROWS + t * GROUP, f * FINAL_ROWS + (t + 1) * GROUP)
+    for t in range(CHUNKS):
+        for copy in share_copies[t]:
+            copy.wait_recv()
+        for k in range(CHUNK // GROUP):
+            at = slice(t * CHUNK + k * GROUP, t * CHUNK + (k + 1) * GROUP)
             stacked = shares[:, at].reshape(N_RET * ENTRIES * GROUP, QUARTER)
             summed = dot(selector, stacked)
             owned[:, at] = summed.astype(BF16).reshape(N_HEAD * POOL_DEV, GROUP, QUARTER)
-        here = pl.ds(f * FINAL_ROWS, FINAL_ROWS)
+        here = pl.ds(t * CHUNK, CHUNK)
         for d in (2, 1, 3):
             own_copies.append(send(
                 owned.at[pl.ds(over_head(d) * POOL_DEV, POOL_DEV), here], oenc.at[:, here, my_columns],
-                s_own.at[f * 3 + d - 1], r_own.at[f * 3 + d - 1], (c, over_head(d), r),
+                s_own.at[t * 3 + d - 1], r_own.at[t * 3 + d - 1], (c, over_head(d), r),
             ))
         own_kept.append(keep(owned.at[pl.ds(h * POOL_DEV, POOL_DEV), here], oenc.at[:, here, my_columns]))
 
@@ -400,9 +421,19 @@
         copy.wait()
     for copy in back_copies + own_copies:
         copy.wait_recv()
-    sent.extend(back_copies + own_copies)
-    for copy in sent:
+    for copy in every:
         copy.wait_send()
+
+
+def place_outputs(*refs):
+    sources, targets, sem = refs[:5], refs[5:10], refs[10]
+    copies = [pltpu.make_async_copy(sources[i], targets[i], sem.at[i]) for i in range(4)]
+    for b in range(POOL_DEV):
+        copies.append(pltpu.make_async_copy(sources[4].at[b], targets[4].at[b], sem.at[4 + b]))
+    for copy in copies:
+        copy.start()
+    for copy in copies:
+        copy.wait()
 
 
 def on_device(
@@ -410,10 +441,11 @@
     neighbours, encodings, key_weight, value_weight,
 ):
     block = jax.ShapeDtypeStruct(self_query.shape, BF16)
-    any_space = pl.BlockSpec(memory_space=pltpu.HBM)
-    in_specs = [any_space] * 11
+    any_space = pl.BlockSpec(memory_space=pl.ANY)
+    in_specs = [pl.BlockSpec(memory_space=pltpu.HBM)] * 11
     in_specs[7] = pl.BlockSpec(memory_space=pltpu.SMEM)
     dma = pltpu.SemaphoreType.DMA
+    wide = (ENTRIES, NR, key_weight.shape[1])
     scratch = [
         pltpu.VMEM((N_RET, 8, 128), jnp.int32),
         pltpu.SMEM((N_RET, 8, 128), jnp.int32),
@@ -432,9 +464,14 @@
         pltpu.VMEM(cross_query.shape[1:], BF16),
         pltpu.VMEM(cross_grad.shape[1:], BF16),
         pltpu.VMEM(cross_grad.shape[1:], BF16),
-        pltpu.VMEM((NBR * NR, E), F32),
-        pltpu.VMEM((N_HEAD, ENTRIES * NR, QUARTER), BF16),
-        pltpu.VMEM((N_HEAD, ENTRIES * NR, QUARTER), BF16),
+        pltpu.VMEM(wide, F32),
+        pltpu.VMEM(wide, F32),
+        pltpu.VMEM(wide, BF16),
+        pltpu.VMEM(wide, BF16),
+        pltpu.VMEM(wide, BF16),
+        pltpu.VMEM(wide, BF16),
+        pltpu.VMEM((N_HEAD, ENTRIES, NR, QUARTER), BF16),
+        pltpu.VMEM((N_HEAD, ENTRIES, NR, QUARTER), BF16),
         pltpu.VMEM((N_RET * ENTRIES, NR, QUARTER), BF16),
         pltpu.VMEM((N_HEAD * POOL_DEV, NR, QUARTER), BF16),
         dma((24,)),
@@ -444,25 +481,36 @@
         dma((3 * CHUNKS,)), dma((3 * CHUNKS,)),
         dma((3 * CHUNKS,)), dma((3 * CHUNKS,)),
         dma((28,)), dma((28,)),
-        dma((6,)), dma((6,)),
-        dma((6,)), dma((6,)),
-        dma((3 * FINAL,)), dma((3 * FINAL,)),
+        dma((3 * CHUNKS,)), dma((3 * CHUNKS,)),
+        dma((3 * CHUNKS,)), dma((3 * CHUNKS,)),
+        dma((3 * CHUNKS,)), dma((3 * CHUNKS,)),
         dma((21,)), dma((21,)),
     ]
-    return pl.pallas_call(
+    outs = pl.pallas_call(
         kernel,
         out_shape=(block, block, block, block, jax.ShapeDtypeStruct(encodings.shape, BF16)),
         in_specs=in_specs,
         out_specs=(any_space,) * 5,
         scratch_shapes=scratch,
         compiler_params=pltpu.CompilerParams(
-            collective_id=0, has_side_effects=True, vmem_limit_bytes=64 * 2**20
+            collective_id=0, has_side_effects=True, vmem_limit_bytes=32 * 2**20
         ),
         name="retro_backward",
-    )(
-        self_query, self_key, self_value, self_grad, self_docs, cross_query, cross_grad,
-        neighbours, encodings, key_weight, value_weight,
-    )
+    )(*[
+        pltpu.with_memory_space_constraint(array, pltpu.HBM)
+        for array in (self_query, self_key, self_value, self_grad, self_docs, cross_query, cross_grad)
+    ], pltpu.with_memory_space_constraint(neighbours, pltpu.SMEM), *[
+        pltpu.with_memory_space_constraint(array, pltpu.HBM)
+        for array in (encodings, key_weight, value_weight)
+    ])
+    return pl.pallas_call(
+        place_outputs,
+        out_shape=(block, block, block, block, jax.ShapeDtypeStruct(encodings.shape, BF16)),
+        in_specs=[any_space] * 5,
+        out_specs=(pl.BlockSpec(memory_space=pltpu.HBM),) * 5,
+        scratch_shapes=[dma((4 + POOL_DEV,))],
+        name="place_outputs",
+    )(*[pltpu.with_memory_space_constraint(out, pltpu.VMEM) for out in outs])
 
 
 def solution(mesh):

time: 73.9 us -> 65.2 us (0.88)
  local copies, waits for them, and re-layouts: 5.87 us -> 0.67 us
  Pallas kernels: 66.2 us -> 62.7 us
    unnamed x11 -> x2, local copies, waits for them, and re-layouts: 5.87 us -> 0.67 us
    pallas_call x1, Pallas kernels: 66.2 us -> 61.3 us  [on_device(): pl.pallas_call(kernel, out_shape=(block, block, block, block, jax.ShapeDt...]
    pallas_call x0 -> x1, Pallas kernels: none -> 1.41 us  [on_device(): pl.pallas_call(place_outputs, out_shape=(block, block, block, block, jax....]
where the time goes in v1:
time: 65.2 us; the launch traced here: 64 us
  Pallas kernels  62.7 us (96%)
  local copies, waits for them, and re-layouts  0.67 us (1%)
    pallas_call x1, Pallas kernels, on_device(): pl.pallas_call(kernel, out_shape=(block, block, block, block, jax.ShapeDt...  61.3 us
    pallas_call x1, Pallas kernels, on_device(): pl.pallas_call(place_outputs, out_shape=(block, block, block, block, jax....  1.41 us

profile of v1, /device:TPU:0, one launch (start us, length us, event | category | flops | bytes accessed | tf_op | source)
XLA Modules:
  0.0 64.0 jit_solution(14349049786381172154)
XLA Ops:
  0.6 0.0 copy-start
  0.6 0.7 %copy-done = s32[1,2,2]{2,1,0:T(2,128)S(1)} copy-done((s32[1,2,2]{2,1,0:T(2,128)S(1)}, s32[1,2,2]{2,1,0:T(2,128)}, u32[]{:S(2)}) %copy-start) | copy-done | bytes 40
  1.3 61.3 %retro_backward.1 = (bf16[1,128,1024]{2,1,0:T(8,128)(2,1)S(1)}, bf16[1,128,1024]{2,1,0:T(8,128)(2,1)S(1)}, bf16[1,128,1024]{2,1,0:T(8,128)(2,1)S(1)}, bf16[1,128...) custom-call(bf16[1,128,1024]{2,1,0:T(8,128)(2,1)} %sq.1, bf16[1,128,1024]{2,1,0:T(8,128)(2,1)} %sk.1, ...), custom_call_target="tpu_custom_call" | custom-call | tf_op jit(solution)/shard_map/retro_backward/pallas_call | solution.py:489
  62.6 1.4 %place_outputs.1 = (bf16[1,128,1024]{2,1,0:T(8,128)(2,1)}, bf16[1,128,1024]{2,1,0:T(8,128)(2,1)}, bf16[1,128,1024]{2,1,0:T(8,128)(2,1)}, bf16[1,128,1024]{2,1,0:T(8,128)(2,1)}, bf16[8,128,512]{2,1,0:T(8,128)(2,1)}) custom-call(bf16[1,128,1024]{2,1,0:T(8,128)(2,1)S(1)} %get-tuple-element.10.refs_0_, bf16[1,128,1024]{2,1,0:T(8,128)(2,1)S(1)} %get-tuple-element.11.refs_1_, ...), custom_call_target="tpu_custom_call" | custom-call | tf_op jit(solution)/shard_map/place_outputs/pallas_call | solution.py:506
Async XLA Ops:
  0.6 0.7 %copy-start = (s32[1,2,2]{2,1,0:T(2,128)S(1)}, s32[1,2,2]{2,1,0:T(2,128)}, u32[]{:S(2)}) copy-start(s32[1,2,2]{2,1,0:T(2,128)} %nbr.1) | copy-start | bytes 52

commit v2 on v1

v2 whole, which is shorter than its diff:
```python
import functools
import math

import jax
import jax.numpy as jnp
from jax import lax
from jax.experimental import pallas as pl
from jax.experimental.pallas import tpu as pltpu
from jax.sharding import PartitionSpec as P

SPAN = 64
NBR = 2
NR = 128
E = 512
DH = 128
POOL_DEV = 8
EPSILON = 1e-06
SCALE = 1.0 / math.sqrt(DH)

N_CTX = 8
N_HEAD = 4
N_RET = 4
ENTRIES = 4
BLOCK = 128
TILE = 256
QUARTER = E // N_HEAD
CHUNKS = 4
ORDER_BACK = (4, 5, 7, 6, 1, 3, 2)
CHUNK = NR // CHUNKS

MESH = pl.DeviceIdType.MESH
F32 = jnp.float32
BF16 = jnp.bfloat16


def dot(a, b):
    return lax.dot_general(a, b, (((1,), (0,)), ((), ())), preferred_element_type=F32)


def dot_nt(a, b):
    return lax.dot_general(a, b, (((1,), (1,)), ((), ())), preferred_element_type=F32)


def kernel(
    sq, sk, sv, sg, docs, cq, cg, nbr, enc, wk, wv,
    oq, ok, ov, ocq, oenc,
    nbr_s, lists_v, lists_s, docs_v, doc_cols, pool, outgoing, incoming, rows, held, key_acc, value_acc, grads,
    wk_v, wv_v, cq_v, cg_v, cross_out, keys_n, factors, keys_b, values_b, raw_grads, value_grads, parts_out, parts_in, shares, owned, selector,
    loc, s_list, r_list, s_docs, r_docs, s_pool, r_pool, s_ret, r_ret, s_rows, r_rows, s_self, r_self,
    s_part, r_part, s_share, r_share, s_own, r_own, s_back, r_back,
):
    c, h, r = lax.axis_index("ctx"), lax.axis_index("head"), lax.axis_index("ret")

    def over_ctx(d):
        return lax.rem(c + d, N_CTX)

    def ctx_peer(d):
        far, step = divmod(d, 4)
        half = lax.rem(lax.div(c, 4) + far, 2)
        return half * 4 + lax.rem(lax.rem(c, 4) + step, 4)

    def over_head(d):
        return lax.rem(h + d, N_HEAD)

    def over_ret(d):
        return lax.rem(r + d, N_RET)

    def send(src, dst, ssem, rsem, device):
        copy = pltpu.make_async_remote_copy(
            src_ref=src, dst_ref=dst, send_sem=ssem, recv_sem=rsem,
            device_id=device, device_id_type=MESH,
        )
        copy.start()
        every.append(copy)
        return copy

    every = []
    local_count = [0]

    def keep(src, dst):
        copy = pltpu.make_async_copy(src, dst, loc.at[local_count[0]])
        local_count[0] += 1
        copy.start()
        return copy

    wanted_copy = keep(nbr, nbr_s)
    barrier = pltpu.get_barrier_semaphore()
    peers = [(over_ctx(d), h, r) for d in range(1, N_CTX)]
    peers += [(c, over_head(d), r) for d in range(1, N_HEAD)]
    peers += [(c, h, over_ret(d)) for d in range(1, N_RET)]
    for peer in peers:
        pl.semaphore_signal(barrier, inc=1, device_id=peer, device_id_type=MESH)
    wanted_copy.wait()
    lane = lax.broadcasted_iota(jnp.int32, (8, 128), 1)
    tile = jnp.zeros((8, 128), jnp.int32)
    for e in range(ENTRIES):
        tile = jnp.where(lane == e, nbr_s[0, e // NBR, e % NBR], tile)
    lists_v[r] = tile
    pl.semaphore_wait(barrier, len(peers))

    def quarter_of(owner_column, t):
        return enc.at[:, pl.ds(t * CHUNK, CHUNK), pl.ds(pl.multiple_of(owner_column * QUARTER, 128), QUARTER)]

    pool_copies = []
    pool_own = []
    for t in range(CHUNKS):
        pool_copies.append([
            send(
                quarter_of(over_head(d), t),
                pool[t].at[pl.ds(h * POOL_DEV, POOL_DEV)],
                s_pool.at[t * 3 + d - 1], r_pool.at[t * 3 + d - 1], (c, over_head(d), r),
            )
            for d in (1, 3, 2)
        ])
        if t == 0:
            list_copies = [
                send(lists_v.at[r], lists_v.at[r], s_list.at[d - 1], r_list.at[d - 1], (c, h, over_ret(d)))
                for d in range(1, N_RET)
            ]
    for t in range(CHUNKS):
        pool_own.append(
            keep(quarter_of(h, t), pool[t].at[pl.ds(h * POOL_DEV, POOL_DEV)])
        )
    doc_copies = [
        send(docs, docs_v.at[c], s_docs.at[d - 1], r_docs.at[d - 1], (over_ctx(d), h, r))
        for d in range(1, N_CTX)
    ]
    doc_own = keep(docs, docs_v.at[c])
    self_in = (sq, sk, sv, sg)

    def head_of(array, number):
        return array.at[0, :, pl.ds(pl.multiple_of(number * DH, 128), DH)]

    self_copies = []
    self_own = []

    def self_start(order):
        for d in order:
            for a in range(4):
                at = (d - 1) * 4 + a
                self_copies.append(send(
                    head_of(self_in[a], ctx_peer(d)),
                    held.at[a, pl.ds(pl.multiple_of(c * BLOCK, 128), BLOCK)],
                    s_self.at[at], r_self.at[at], (ctx_peer(d), h, r),
                ))

    def self_keep():
        for a in range(4):
            self_own.append(
                keep(head_of(self_in[a], c), held.at[a, pl.ds(pl.multiple_of(c * BLOCK, 128), BLOCK)])
            )

    self_start((1, 3, 2))
    self_keep()
    cross_own = [keep(wk, wk_v), keep(wv, wv_v), keep(cq.at[0], cq_v), keep(cg.at[0], cg_v)]

    for copy in list_copies:
        copy.wait_recv()
    to_scalars = keep(lists_v, lists_s)
    to_scalars.wait()

    ret_copies = []
    row_copies = []
    my_columns = pl.ds(pl.multiple_of(h * QUARTER, 128), QUARTER)

    def hand_out(t):
        here = pl.ds(t * CHUNK, CHUNK)
        pool_own[t].wait()
        for copy in pool_copies[t]:
            copy.wait_recv()
        for q in range(N_RET):
            for e in range(ENTRIES):
                value = lists_s[q, 0, e]
                place = lax.div(value, N_RET * POOL_DEV) * POOL_DEV + lax.rem(value, POOL_DEV)
                outgoing[q * ENTRIES + e, here] = pool[t][place]
        ret_copies.append([
            send(
                outgoing.at[pl.ds(over_ret(d) * ENTRIES, ENTRIES), here],
                incoming[t].at[pl.ds(r * ENTRIES, ENTRIES)],
                s_ret.at[t * 3 + d - 1], r_ret.at[t * 3 + d - 1], (c, h, over_ret(d)),
            )
            for d in (1, 3, 2)
        ])
        incoming[t][pl.ds(r * ENTRIES, ENTRIES)] = outgoing[pl.ds(r * ENTRIES, ENTRIES), here]

    def spread(t):
        here = pl.ds(t * CHUNK, CHUNK)
        for copy in ret_copies[t]:
            copy.wait_recv()
        for e in range(ENTRIES):
            value = lists_s[r, 0, e]
            column = lax.rem(lax.div(value, POOL_DEV), N_RET)
            rows[e, here, my_columns] = incoming[t][column * ENTRIES + e]
        row_copies.append([
            send(
                rows.at[:, here, my_columns], rows.at[:, here, my_columns],
                s_rows.at[t * 3 + d - 1], r_rows.at[t * 3 + d - 1], (c, over_head(d), r),
            )
            for d in (1, 3, 2)
        ])

    for t in range(CHUNKS + 1):
        if t < CHUNKS:
            hand_out(t)
        if t == CHUNKS - 1:
            self_start((4, 5, 7, 6))
        if t >= 1:
            spread(t - 1)

    GROUP = 16
    lane_e = lax.broadcasted_iota(jnp.int32, (1, N_RET * ENTRIES * GROUP), 1)
    named = jnp.zeros((1, N_RET * ENTRIES * GROUP), jnp.int32)
    for q in range(N_RET):
        for e in range(ENTRIES):
            k = q * ENTRIES + e
            named = jnp.where(lane_e // GROUP == k, lists_s[q, 0, e], named)
    wide = (N_HEAD * POOL_DEV * GROUP, N_RET * ENTRIES * GROUP)
    target = lax.broadcasted_iota(jnp.int32, wide, 0)
    slot = target // GROUP
    wanted = ((slot // POOL_DEV) * N_RET + r) * POOL_DEV + slot % POOL_DEV
    same_token = target % GROUP == lax.broadcasted_iota(jnp.int32, wide, 1) % GROUP
    selector[...] = jnp.where((wanted == named) & same_token, 1.0, 0.0).astype(BF16)

    def prepare_self():
        doc_own.wait()
        for copy in doc_copies + self_copies:
            copy.wait_recv()
        for copy in self_own:
            copy.wait()
        for b in range(N_CTX):
            one = jnp.broadcast_to(docs_v[b].astype(F32), (BLOCK, BLOCK))
            doc_cols[b * BLOCK:(b + 1) * BLOCK] = one.T

    key_at = lax.broadcasted_iota(jnp.int32, (TILE, TILE), 0)
    query_at = lax.broadcasted_iota(jnp.int32, (TILE, TILE), 1)

    def self_rows(i):
        mine = slice(i * TILE, (i + 1) * TILE)
        query, grad = held[0, mine], held[3, mine]
        query_docs = jnp.concatenate([docs_v[2 * i], docs_v[2 * i + 1]], axis=1).astype(F32)
        first = max(0, i - 2)
        totals = jnp.zeros((1, TILE), F32)
        deltas = jnp.zeros((1, TILE), F32)
        raws, dnormeds = [], []
        for j in range(first, i + 1):
            there = slice(j * TILE, (j + 1) * TILE)
            key_docs = doc_cols[there]
            visible = jnp.concatenate([key_docs, key_docs], axis=1) == query_docs
            if j == i:
                visible = visible & (key_at <= query_at)
            raw = jnp.where(visible, jnp.exp(dot_nt(held[1, there], query) * SCALE), 0.0)
            dnormed = dot_nt(held[2, there], grad)
            totals = totals + jnp.sum(raw, axis=0, keepdims=True)
            deltas = deltas + jnp.sum(raw.astype(BF16).astype(F32) * dnormed, axis=0, keepdims=True)
            raws.append(raw)
            dnormeds.append(dnormed)
        inverse = 1.0 / totals
        deltas = deltas * inverse
        query_sum = jnp.zeros((DH, TILE), F32)
        for j in range(first, i + 1):
            there = slice(j * TILE, (j + 1) * TILE)
            normed = raws[j - first] * inverse
            dscores = (normed * (dnormeds[j - first] - deltas)).astype(BF16)
            query_sum = query_sum + dot(held[1, there].astype(F32).T.astype(BF16), dscores)
            key_term = dot(dscores, query)
            value_term = dot(normed.astype(BF16), grad)
            if j == i:
                key_acc[there] = key_term
                value_acc[there] = value_term
            else:
                key_acc[there] += key_term
                value_acc[there] += value_term
        grads[0, mine] = (query_sum * SCALE).T.astype(BF16)

    def self_finish():
        grads[1] = (key_acc[...] * SCALE).astype(BF16)
        grads[2] = value_acc[...].astype(BF16)

    def self_back():
        outs = (oq, ok, ov)
        copies = []
        for d in ORDER_BACK:
            for a in range(3):
                at = (d - 1) * 3 + a
                copies.append(send(
                    grads.at[a, pl.ds(pl.multiple_of(ctx_peer(d) * BLOCK, 128), BLOCK)],
                    head_of(outs[a], c),
                    s_back.at[at], r_back.at[at], (ctx_peer(d), h, r),
                ))
        own = [
            keep(grads.at[a, pl.ds(pl.multiple_of(c * BLOCK, 128), BLOCK)], head_of(outs[a], c))
            for a in range(3)
        ]
        return copies, own

    for copy in cross_own:
        copy.wait()

    def pieces(width):
        return [slice(n * width, (n + 1) * width) for n in range(keys_b.shape[2] // width)]

    def project(t):
        here = slice(t * CHUNK, (t + 1) * CHUNK)
        for copy in row_copies[t]:
            copy.wait_recv()
        tokens = rows[:, here, :].reshape(ENTRIES * CHUNK, E)
        for cols in pieces(TILE):
            keys_raw = dot(tokens, wk_v[:, cols])
            values_b[:, here, cols] = dot(tokens, wv_v[:, cols]).astype(BF16).reshape(ENTRIES, CHUNK, TILE)
            for a in range(2):
                one = keys_raw[:, a * DH:(a + 1) * DH]
                mean = jnp.sum(one * one, axis=1, keepdims=True) * (1.0 / DH)
                factor = jnp.broadcast_to(lax.rsqrt(mean + EPSILON), one.shape)
                normed = one * factor
                at = slice(cols.start + a * DH, cols.start + (a + 1) * DH)
                factors[:, here, at] = factor.reshape(ENTRIES, CHUNK, DH)
                keys_n[:, here, at] = normed.reshape(ENTRIES, CHUNK, DH)
                keys_b[:, here, at] = normed.astype(BF16).reshape(ENTRIES, CHUNK, DH)

    for t in range(CHUNKS):
        project(t)

    lanes = lax.broadcasted_iota(jnp.int32, (SPAN, TILE), 1)

    def paired(block):
        low = jnp.where(lanes < DH, block, jnp.zeros_like(block))
        high = jnp.where(lanes >= DH, block, jnp.zeros_like(block))
        return jnp.concatenate([low, high], axis=0)

    def attend(s):
        here = slice(s * SPAN, (s + 1) * SPAN)
        mine = slice(s * NBR, (s + 1) * NBR)
        pairs = pieces(TILE)

        def span_of(array, cols):
            return array[mine, :, cols].reshape(NBR * NR, cols.stop - cols.start)

        queries = [paired(cq_v[here, cols]) for cols in pairs]
        outer = [paired(cg_v[here, cols]) for cols in pairs]
        raws = [jnp.exp(dot_nt(span_of(keys_b, cols), q) * SCALE) for cols, q in zip(pairs, queries)]
        dprobs = [dot_nt(span_of(values_b, cols), g) for cols, g in zip(pairs, outer)]
        probs = [raw * (1.0 / jnp.sum(raw, axis=0, keepdims=True)) for raw in raws]
        probs_b = [p.astype(BF16) for p in probs]
        cdeltas = [jnp.sum(p.astype(F32) * d, axis=0, keepdims=True) for p, d in zip(probs_b, dprobs)]
        dscores = [p * (d - c) for p, d, c in zip(probs, dprobs, cdeltas)]
        dscores_b = [d.astype(BF16) for d in dscores]
        grad_keys = [dot(d, q) * SCALE for d, q in zip(dscores_b, queries)]
        for cols, p, g in zip(pairs, probs_b, outer):
            value_grads[mine, :, cols] = dot(p, g).astype(BF16).reshape(NBR, NR, TILE)
        for cols, d in zip(pairs, dscores):
            part = dot(d.T.astype(BF16), span_of(keys_b, cols)) * SCALE
            cross_out[here, cols.start:cols.start + DH] = part[:SPAN, :DH].astype(BF16)
            cross_out[here, cols.start + DH:cols.stop] = part[SPAN:, DH:].astype(BF16)
        for cols, grad in zip(pairs, grad_keys):
            for a in range(2):
                at = slice(cols.start + a * DH, cols.start + (a + 1) * DH)
                one = grad[:, a * DH:(a + 1) * DH]
                normed = span_of(keys_n, at)
                mean = jnp.sum(normed * one, axis=1, keepdims=True) * (1.0 / DH)
                raw = span_of(factors, at) * (one - normed * mean)
                raw_grads[mine, :, at] = raw.astype(BF16).reshape(NBR, NR, DH)

    for s in range(2):
        attend(s)
    cross_done = keep(cross_out, ocq.at[0])

    def scatter(t):
        here = pl.ds(t * CHUNK, CHUNK)
        shape = (ENTRIES * CHUNK, keys_b.shape[2])
        term = dot_nt(raw_grads[:, here, :].reshape(shape), wk_v[...])
        term = term + dot_nt(value_grads[:, here, :].reshape(shape), wv_v[...])
        for q in range(N_HEAD):
            one = term[:, q * QUARTER:(q + 1) * QUARTER].astype(BF16)
            parts_out[q, :, here, :] = one.reshape(ENTRIES, CHUNK, QUARTER)
        return [
            send(
                parts_out.at[over_head(d), :, here], parts_in.at[h, :, here],
                s_part.at[t * 3 + d - 1], r_part.at[t * 3 + d - 1], (c, over_head(d), r),
            )
            for d in (1, 3, 2)
        ]

    part_copies = [scatter(t) for t in range(CHUNKS)]

    def share(t):
        here = pl.ds(t * CHUNK, CHUNK)
        for copy in part_copies[t]:
            copy.wait_recv()
        total = parts_out[h, :, here, :].astype(F32)
        for d in range(1, N_HEAD):
            total = total + parts_in[over_head(d), :, here, :].astype(F32)
        mine = pl.ds(r * ENTRIES, ENTRIES)
        shares[mine, here] = total.astype(BF16)
        return [
            send(
                shares.at[mine, here], shares.at[mine, here],
                s_share.at[t * 3 + d - 1], r_share.at[t * 3 + d - 1], (c, h, over_ret(d)),
            )
            for d in (1, 3, 2)
        ]

    own_copies = []
    own_kept = []

    def hand_back(t):
        for copy in share_copies[t]:
            copy.wait_recv()
        for k in range(CHUNK // GROUP):
            at = slice(t * CHUNK + k * GROUP, t * CHUNK + (k + 1) * GROUP)
            stacked = shares[:, at].reshape(N_RET * ENTRIES * GROUP, QUARTER)
            summed = dot(selector[...], stacked)
            owned[:, at] = summed.astype(BF16).reshape(N_HEAD * POOL_DEV, GROUP, QUARTER)
        here = pl.ds(t * CHUNK, CHUNK)
        for d in (1, 3, 2):
            own_copies.append(send(
                owned.at[pl.ds(over_head(d) * POOL_DEV, POOL_DEV), here], oenc.at[:, here, my_columns],
                s_own.at[t * 3 + d - 1], r_own.at[t * 3 + d - 1], (c, over_head(d), r),
            ))
        own_kept.append(keep(owned.at[pl.ds(h * POOL_DEV, POOL_DEV), here], oenc.at[:, here, my_columns]))

    back_copies, back_own = [], []
    share_copies = []
    prepare_self()
    self_rows(0)
    self_rows(1)
    share_copies.append(share(0))
    share_copies.append(share(1))
    self_rows(2)
    share_copies.append(share(2))
    share_copies.append(share(3))
    hand_back(0)
    self_rows(3)
    self_finish()
    hand_back(1)
    back_copies, back_own = self_back()
    hand_back(2)
    hand_back(3)

    cross_done.wait()
    for copy in back_own + own_kept:
        copy.wait()
    for copy in back_copies + own_copies:
        copy.wait_recv()
    for copy in every:
        copy.wait_send()


def place_outputs(*refs):
    sources, targets, sem = refs[:5], refs[5:10], refs[10]
    copies = [pltpu.make_async_copy(sources[i], targets[i], sem.at[i]) for i in range(4)]
    for b in range(POOL_DEV):
        copies.append(pltpu.make_async_copy(sources[4].at[b], targets[4].at[b], sem.at[4 + b]))
    for copy in copies:
        copy.start()
    for copy in copies:
        copy.wait()


def on_device(
    self_query, self_key, self_value, self_grad, self_docs, cross_query, cross_grad,
    neighbours, encodings, key_weight, value_weight,
):
    block = jax.ShapeDtypeStruct(self_query.shape, BF16)
    any_space = pl.BlockSpec(memory_space=pl.ANY)
    in_specs = [pl.BlockSpec(memory_space=pltpu.HBM)] * 11
    dma = pltpu.SemaphoreType.DMA
    wide = (ENTRIES, NR, key_weight.shape[1])
    scratch = [
        pltpu.SMEM(neighbours.shape, jnp.int32),
        pltpu.VMEM((N_RET, 8, 128), jnp.int32),
        pltpu.SMEM((N_RET, 8, 128), jnp.int32),
        pltpu.VMEM((N_CTX, 1, BLOCK), jnp.int32),
        pltpu.VMEM((N_CTX * BLOCK, 128), F32),
        (pltpu.VMEM((N_HEAD * POOL_DEV, CHUNK, QUARTER), BF16),) * CHUNKS,
        pltpu.VMEM((N_RET * ENTRIES, NR, QUARTER), BF16),
        (pltpu.VMEM((N_RET * ENTRIES, CHUNK, QUARTER), BF16),) * CHUNKS,
        pltpu.VMEM((ENTRIES, NR, E), BF16),
        pltpu.VMEM((4, N_CTX * BLOCK, DH), BF16),
        pltpu.VMEM((N_CTX * BLOCK, DH), F32),
        pltpu.VMEM((N_CTX * BLOCK, DH), F32),
        pltpu.VMEM((3, N_CTX * BLOCK, DH), BF16),
        pltpu.VMEM(key_weight.shape, BF16),
        pltpu.VMEM(value_weight.shape, BF16),
        pltpu.VMEM(cross_query.shape[1:], BF16),
        pltpu.VMEM(cross_grad.shape[1:], BF16),
        pltpu.VMEM(cross_grad.shape[1:], BF16),
        pltpu.VMEM(wide, F32),
        pltpu.VMEM(wide, F32),
        pltpu.VMEM(wide, BF16),
        pltpu.VMEM(wide, BF16),
        pltpu.VMEM(wide, BF16),
        pltpu.VMEM(wide, BF16),
        pltpu.VMEM((N_HEAD, ENTRIES, NR, QUARTER), BF16),
        pltpu.VMEM((N_HEAD, ENTRIES, NR, QUARTER), BF16),
        pltpu.VMEM((N_RET * ENTRIES, NR, QUARTER), BF16),
        pltpu.VMEM((N_HEAD * POOL_DEV, NR, QUARTER), BF16),
        pltpu.VMEM((N_HEAD * POOL_DEV * 16, N_RET * ENTRIES * 16), BF16),
        dma((32,)),
        dma((3,)), dma((3,)),
        dma((7,)), dma((7,)),
        dma((3 * CHUNKS,)), dma((3 * CHUNKS,)),
        dma((3 * CHUNKS,)), dma((3 * CHUNKS,)),
        dma((3 * CHUNKS,)), dma((3 * CHUNKS,)),
        dma((28,)), dma((28,)),
        dma((3 * CHUNKS,)), dma((3 * CHUNKS,)),
        dma((3 * CHUNKS,)), dma((3 * CHUNKS,)),
        dma((3 * CHUNKS,)), dma((3 * CHUNKS,)),
        dma((21,)), dma((21,)),
    ]
    outs = pl.pallas_call(
        kernel,
        out_shape=(block, block, block, block, jax.ShapeDtypeStruct(encodings.shape, BF16)),
        in_specs=in_specs,
        out_specs=(any_space,) * 5,
        scratch_shapes=scratch,
        compiler_params=pltpu.CompilerParams(
            collective_id=0, has_side_effects=True, vmem_limit_bytes=32 * 2**20
        ),
        name="retro_backward",
    )(*[
        pltpu.with_memory_space_constraint(array, pltpu.HBM)
        for array in (self_query, self_key, self_value, self_grad, self_docs, cross_query, cross_grad)
    ], pltpu.with_memory_space_constraint(neighbours, pltpu.HBM), *[
        pltpu.with_memory_space_constraint(array, pltpu.HBM)
        for array in (encodings, key_weight, value_weight)
    ])
    return pl.pallas_call(
        place_outputs,
        out_shape=(block, block, block, block, jax.ShapeDtypeStruct(encodings.shape, BF16)),
        in_specs=[any_space] * 5,
        out_specs=(pl.BlockSpec(memory_space=pltpu.HBM),) * 5,
        scratch_shapes=[dma((4 + POOL_DEV,))],
        name="place_outputs",
    )(*[pltpu.with_memory_space_constraint(out, pltpu.VMEM) for out in outs])


def solution(mesh):
    tokens = P("ret", "ctx", "head")
    pool = P(("ctx", "head", "ret"), None, None)
    placed = (
        tokens, tokens, tokens, tokens, P("ret", "ctx"), tokens, tokens,
        P("ret", "ctx", None), pool, P(None, "head"), P(None, "head"),
    )
    return jax.shard_map(
        on_device,
        mesh=mesh,
        in_specs=placed,
        out_specs=(tokens, tokens, tokens, tokens, pool),
        check_vma=False,
    )
```

time: 65.2 us -> 61.1 us (0.937); the launches traced: 64 us -> 61 us
  Pallas kernels: 62.7 us -> 60.3 us
  local copies, waits for them, and re-layouts: 0.67 us -> 0 us
    pallas_call x1, Pallas kernels: 61.3 us -> 58.9 us  [on_device(): pl.pallas_call(kernel, out_shape=(block, block, block, block, jax.ShapeDt...]
    unnamed x2 -> x0, local copies, waits for them, and re-layouts: 0.67 us -> none
where the time goes in v2:
time: 61.1 us; the launch traced here: 61 us
  Pallas kernels  60.3 us (99%)
  between operations  0.64 us (1%)
    pallas_call x1, Pallas kernels, on_device(): pl.pallas_call(kernel, out_shape=(block, block, block, block, jax.ShapeDt...  58.9 us
    pallas_call x1, Pallas kernels, on_device(): pl.pallas_call(place_outputs, out_shape=(block, block, block, block, jax....  1.41 us

profile of v2, /device:TPU:0, one launch (start us, length us, event | category | flops | bytes accessed | tf_op | source)
XLA Modules:
  0.0 61.0 jit_solution(2012288802846191836)
XLA Ops:
  0.6 58.9 %retro_backward.1 = (bf16[1,128,1024]{2,1,0:T(8,128)(2,1)S(1)}, bf16[1,128,1024]{2,1,0:T(8,128)(2,1)S(1)}, bf16[1,128,1024]{2,1,0:T(8,128)(2,1)S(1)}, bf16[1,128...) custom-call(bf16[1,128,1024]{2,1,0:T(8,128)(2,1)} %sq.1, bf16[1,128,1024]{2,1,0:T(8,128)(2,1)} %sk.1, ...), custom_call_target="tpu_custom_call" | custom-call | tf_op jit(solution)/shard_map/retro_backward/pallas_call | solution.py:510
  59.6 1.4 %place_outputs.1 = (bf16[1,128,1024]{2,1,0:T(8,128)(2,1)}, bf16[1,128,1024]{2,1,0:T(8,128)(2,1)}, bf16[1,128,1024]{2,1,0:T(8,128)(2,1)}, bf16[1,128,1024]{2,1,0:T(8,128)(2,1)}, bf16[8,128,512]{2,1,0:T(8,128)(2,1)}) custom-call(bf16[1,128,1024]{2,1,0:T(8,128)(2,1)S(1)} %get-tuple-element.10.refs_0_, bf16[1,128,1024]{2,1,0:T(8,128)(2,1)S(1)} %get-tuple-element.11.refs_1_, ...), custom_call_target="tpu_custom_call" | custom-call | tf_op jit(solution)/shard_map/place_outputs/pallas_call | solution.py:527

commit v3 on v2

--- a/solution.py
+++ b/solution.py
@@ -23,6 +23,7 @@
 ENTRIES = 4
 BLOCK = 128
 TILE = 256
+DOC_ROWS = 16
 QUARTER = E // N_HEAD
 CHUNKS = 4
 ORDER_BACK = (4, 5, 7, 6, 1, 3, 2)
@@ -43,10 +44,10 @@
 
 def kernel(
     sq, sk, sv, sg, docs, cq, cg, nbr, enc, wk, wv,
-    oq, ok, ov, ocq, oenc,
-    nbr_s, lists_v, lists_s, docs_v, doc_cols, pool, outgoing, incoming, rows, held, key_acc, value_acc, grads,
+    oself, ocq, oenc,
+    nbr_s, lists_v, lists_s, docs_v, doc_cols, staged, pool, outgoing, incoming, rows, held, key_acc, value_acc, grads,
     wk_v, wv_v, cq_v, cg_v, cross_out, keys_n, factors, keys_b, values_b, raw_grads, value_grads, parts_out, parts_in, shares, owned, selector,
-    loc, s_list, r_list, s_docs, r_docs, s_pool, r_pool, s_ret, r_ret, s_rows, r_rows, s_self, r_self,
+    loc, s_list, r_list, s_pool, r_pool, s_ret, r_ret, s_rows, r_rows, s_self, r_self,
     s_part, r_part, s_share, r_share, s_own, r_own, s_back, r_back,
 ):
     c, h, r = lax.axis_index("ctx"), lax.axis_index("head"), lax.axis_index("ret")
@@ -75,6 +76,11 @@
         return copy
 
     every = []
+
+    def flush(left):
+        while len(every) > left:
+            every.pop(0).wait_send()
+
     local_count = [0]
 
     def keep(src, dst):
@@ -84,6 +90,10 @@
         return copy
 
     wanted_copy = keep(nbr, nbr_s)
+    doc_copy = keep(docs, docs_v)
+    staging = [
+        keep(array.at[0], staged.at[pl.ds(a * BLOCK, BLOCK)]) for a, array in enumerate((sq, sk, sv, sg))
+    ]
     barrier = pltpu.get_barrier_semaphore()
     peers = [(over_ctx(d), h, r) for d in range(1, N_CTX)]
     peers += [(c, over_head(d), r) for d in range(1, N_HEAD)]
@@ -96,6 +106,10 @@
     for e in range(ENTRIES):
         tile = jnp.where(lane == e, nbr_s[0, e // NBR, e % NBR], tile)
     lists_v[r] = tile
+    doc_copy.wait()
+    doc_rows = jnp.broadcast_to(docs_v[...].astype(F32), (DOC_ROWS, BLOCK)).astype(BF16)
+    for k in range(N_CTX):
+        staged[4 * BLOCK:, k * DH:(k + 1) * DH] = doc_rows
     pl.semaphore_wait(barrier, len(peers))
 
     def quarter_of(owner_column, t):
@@ -121,37 +135,23 @@
         pool_own.append(
             keep(quarter_of(h, t), pool[t].at[pl.ds(h * POOL_DEV, POOL_DEV)])
         )
-    doc_copies = [
-        send(docs, docs_v.at[c], s_docs.at[d - 1], r_docs.at[d - 1], (over_ctx(d), h, r))
-        for d in range(1, N_CTX)
-    ]
-    doc_own = keep(docs, docs_v.at[c])
-    self_in = (sq, sk, sv, sg)
-
-    def head_of(array, number):
-        return array.at[0, :, pl.ds(pl.multiple_of(number * DH, 128), DH)]
-
     self_copies = []
     self_own = []
 
+    def head_columns(number):
+        return pl.ds(pl.multiple_of(number * DH, 128), DH)
+
     def self_start(order):
         for d in order:
-            for a in range(4):
-                at = (d - 1) * 4 + a
-                self_copies.append(send(
-                    head_of(self_in[a], ctx_peer(d)),
-                    held.at[a, pl.ds(pl.multiple_of(c * BLOCK, 128), BLOCK)],
-                    s_self.at[at], r_self.at[at], (ctx_peer(d), h, r),
-                ))
-
-    def self_keep():
-        for a in range(4):
-            self_own.append(
-                keep(head_of(self_in[a], c), held.at[a, pl.ds(pl.multiple_of(c * BLOCK, 128), BLOCK)])
-            )
-
+            self_copies.append(send(
+                staged.at[:, head_columns(ctx_peer(d))], held.at[c],
+                s_self.at[d - 1], r_self.at[d - 1], (ctx_peer(d), h, r),
+            ))
+
+    for copy in staging:
+        copy.wait()
     self_start((1, 3, 2))
-    self_keep()
+    self_own.append(keep(staged.at[:, head_columns(c)], held.at[c]))
     cross_own = [keep(wk, wk_v), keep(wv, wv_v), keep(cq.at[0], cq_v), keep(cg.at[0], cg_v)]
 
     for copy in list_copies:
@@ -159,6 +159,9 @@
     to_scalars = keep(lists_v, lists_s)
     to_scalars.wait()
 
+    entries = [[lists_s[q, 0, e] for e in range(ENTRIES)] for q in range(N_RET)]
+    places = [[(v >> 5) * POOL_DEV + (v & 7) for v in one] for one in entries]
+    wanted_columns = [(lists_s[r, 0, e] >> 3) & 3 for e in range(ENTRIES)]
     ret_copies = []
     row_copies = []
     my_columns = pl.ds(pl.multiple_of(h * QUARTER, 128), QUARTER)
@@ -170,9 +173,7 @@
             copy.wait_recv()
         for q in range(N_RET):
             for e in range(ENTRIES):
-                value = lists_s[q, 0, e]
-                place = lax.div(value, N_RET * POOL_DEV) * POOL_DEV + lax.rem(value, POOL_DEV)
-                outgoing[q * ENTRIES + e, here] = pool[t][place]
+                outgoing[q * ENTRIES + e, here] = pool[t][places[q][e]]
         ret_copies.append([
             send(
                 outgoing.at[pl.ds(over_ret(d) * ENTRIES, ENTRIES), here],
@@ -188,9 +189,7 @@
         for copy in ret_copies[t]:
             copy.wait_recv()
         for e in range(ENTRIES):
-            value = lists_s[r, 0, e]
-            column = lax.rem(lax.div(value, POOL_DEV), N_RET)
-            rows[e, here, my_columns] = incoming[t][column * ENTRIES + e]
+            rows[e, here, my_columns] = incoming[t][wanted_columns[e] * ENTRIES + e]
         row_copies.append([
             send(
                 rows.at[:, here, my_columns], rows.at[:, here, my_columns],
@@ -213,7 +212,7 @@
     for q in range(N_RET):
         for e in range(ENTRIES):
             k = q * ENTRIES + e
-            named = jnp.where(lane_e // GROUP == k, lists_s[q, 0, e], named)
+            named = jnp.where(lane_e // GROUP == k, entries[q][e], named)
     wide = (N_HEAD * POOL_DEV * GROUP, N_RET * ENTRIES * GROUP)
     target = lax.broadcasted_iota(jnp.int32, wide, 0)
     slot = target // GROUP
@@ -221,14 +220,19 @@
     same_token = target % GROUP == lax.broadcasted_iota(jnp.int32, wide, 1) % GROUP
     selector[...] = jnp.where((wanted == named) & same_token, 1.0, 0.0).astype(BF16)
 
+    def doc_row(b):
+        return held[b, 4 * BLOCK:, :].astype(F32)[:1]
+
+    def tokens_of(a, i):
+        return held[2 * i:2 * i + 2, a * BLOCK:(a + 1) * BLOCK, :].reshape(TILE, DH)
+
     def prepare_self():
-        doc_own.wait()
-        for copy in doc_copies + self_copies:
+        for copy in self_copies:
             copy.wait_recv()
         for copy in self_own:
             copy.wait()
         for b in range(N_CTX):
-            one = jnp.broadcast_to(docs_v[b].astype(F32), (BLOCK, BLOCK))
+            one = jnp.broadcast_to(doc_row(b), (BLOCK, BLOCK))
             doc_cols[b * BLOCK:(b + 1) * BLOCK] = one.T
 
     key_at = lax.broadcasted_iota(jnp.int32, (TILE, TILE), 0)
@@ -236,8 +240,8 @@
 
     def self_rows(i):
         mine = slice(i * TILE, (i + 1) * TILE)
-        query, grad = held[0, mine], held[3, mine]
-        query_docs = jnp.concatenate([docs_v[2 * i], docs_v[2 * i + 1]], axis=1).astype(F32)
+        query, grad = tokens_of(0, i), tokens_of(3, i)
+        query_docs = jnp.concatenate([doc_row(2 * i), doc_row(2 * i + 1)], axis=1)
         first = max(0, i - 2)
         totals = jnp.zeros((1, TILE), F32)
         deltas = jnp.zeros((1, TILE), F32)
@@ -248,8 +252,8 @@
             visible = jnp.concatenate([key_docs, key_docs], axis=1) == query_docs
             if j == i:
                 visible = visible & (key_at <= query_at)
-            raw = jnp.where(visible, jnp.exp(dot_nt(held[1, there], query) * SCALE), 0.0)
-            dnormed = dot_nt(held[2, there], grad)
+            raw = jnp.where(visible, jnp.exp(dot_nt(tokens_of(1, j), query) * SCALE), 0.0)
+            dnormed = dot_nt(tokens_of(2, j), grad)
             totals = totals + jnp.sum(raw, axis=0, keepdims=True)
             deltas = deltas + jnp.sum(raw.astype(BF16).astype(F32) * dnormed, axis=0, keepdims=True)
             raws.append(raw)
@@ -261,7 +265,7 @@
             there = slice(j * TILE, (j + 1) * TILE)
             normed = raws[j - first] * inverse
             dscores = (normed * (dnormeds[j - first] - deltas)).astype(BF16)
-            query_sum = query_sum + dot(held[1, there].astype(F32).T.astype(BF16), dscores)
+            query_sum = query_sum + dot(tokens_of(1, j).astype(F32).T.astype(BF16), dscores)
             key_term = dot(dscores, query)
             value_term = dot(normed.astype(BF16), grad)
             if j == i:
@@ -277,21 +281,15 @@
         grads[2] = value_acc[...].astype(BF16)
 
     def self_back():
-        outs = (oq, ok, ov)
         copies = []
         for d in ORDER_BACK:
-            for a in range(3):
-                at = (d - 1) * 3 + a
-                copies.append(send(
-                    grads.at[a, pl.ds(pl.multiple_of(ctx_peer(d) * BLOCK, 128), BLOCK)],
-                    head_of(outs[a], c),
-                    s_back.at[at], r_back.at[at], (ctx_peer(d), h, r),
-                ))
-        own = [
-            keep(grads.at[a, pl.ds(pl.multiple_of(c * BLOCK, 128), BLOCK)], head_of(outs[a], c))
-            for a in range(3)
-        ]
-        return copies, own
+            there = pl.ds(pl.multiple_of(ctx_peer(d) * BLOCK, 128), BLOCK)
+            copies.append(send(
+                grads.at[:, there], oself.at[:, :, head_columns(c)],
+                s_back.at[d - 1], r_back.at[d - 1], (ctx_peer(d), h, r),
+            ))
+        here = pl.ds(pl.multiple_of(c * BLOCK, 128), BLOCK)
+        return copies, [keep(grads.at[:, here], oself.at[:, :, head_columns(c)])]
 
     for copy in cross_own:
         copy.wait()
@@ -420,6 +418,7 @@
 
     back_copies, back_own = [], []
     share_copies = []
+    flush(3 * CHUNKS)
     prepare_self()
     self_rows(0)
     self_rows(1)
@@ -429,6 +428,7 @@
     share_copies.append(share(2))
     share_copies.append(share(3))
     hand_back(0)
+    flush(3 + 3 * CHUNKS)
     self_rows(3)
     self_finish()
     hand_back(1)
@@ -441,15 +441,15 @@
         copy.wait()
     for copy in back_copies + own_copies:
         copy.wait_recv()
-    for copy in every:
-        copy.wait_send()
-
-
-def place_outputs(*refs):
-    sources, targets, sem = refs[:5], refs[5:10], refs[10]
-    copies = [pltpu.make_async_copy(sources[i], targets[i], sem.at[i]) for i in range(4)]
+    flush(0)
+
+
+def place_outputs(own, cross, pool, *refs):
+    targets, sem = refs[:5], refs[5]
+    copies = [pltpu.make_async_copy(own.at[a], targets[a].at[0], sem.at[a]) for a in range(3)]
+    copies.append(pltpu.make_async_copy(cross, targets[3], sem.at[3]))
     for b in range(POOL_DEV):
-        copies.append(pltpu.make_async_copy(sources[4].at[b], targets[4].at[b], sem.at[4 + b]))
+        copies.append(pltpu.make_async_copy(pool.at[b], targets[4].at[b], sem.at[4 + b]))
     for copy in copies:
         copy.start()
     for copy in copies:
@@ -469,13 +469,14 @@
         pltpu.SMEM(neighbours.shape, jnp.int32),
         pltpu.VMEM((N_RET, 8, 128), jnp.int32),
         pltpu.SMEM((N_RET, 8, 128), jnp.int32),
-        pltpu.VMEM((N_CTX, 1, BLOCK), jnp.int32),
+        pltpu.VMEM((1, BLOCK), jnp.int32),
         pltpu.VMEM((N_CTX * BLOCK, 128), F32),
+        pltpu.VMEM((4 * BLOCK + DOC_ROWS, N_CTX * DH), BF16),
         (pltpu.VMEM((N_HEAD * POOL_DEV, CHUNK, QUARTER), BF16),) * CHUNKS,
         pltpu.VMEM((N_RET * ENTRIES, NR, QUARTER), BF16),
         (pltpu.VMEM((N_RET * ENTRIES, CHUNK, QUARTER), BF16),) * CHUNKS,
         pltpu.VMEM((ENTRIES, NR, E), BF16),
-        pltpu.VMEM((4, N_CTX * BLOCK, DH), BF16),
+        pltpu.VMEM((N_CTX, 4 * BLOCK + DOC_ROWS, DH), BF16),
         pltpu.VMEM((N_CTX * BLOCK, DH), F32),
         pltpu.VMEM((N_CTX * BLOCK, DH), F32),
         pltpu.VMEM((3, N_CTX * BLOCK, DH), BF16),
@@ -497,21 +498,23 @@
         pltpu.VMEM((N_HEAD * POOL_DEV * 16, N_RET * ENTRIES * 16), BF16),
         dma((32,)),
         dma((3,)), dma((3,)),
+        dma((3 * CHUNKS,)), dma((3 * CHUNKS,)),
+        dma((3 * CHUNKS,)), dma((3 * CHUNKS,)),
+        dma((3 * CHUNKS,)), dma((3 * CHUNKS,)),
         dma((7,)), dma((7,)),
         dma((3 * CHUNKS,)), dma((3 * CHUNKS,)),
         dma((3 * CHUNKS,)), dma((3 * CHUNKS,)),
         dma((3 * CHUNKS,)), dma((3 * CHUNKS,)),
-        dma((28,)), dma((28,)),
-        dma((3 * CHUNKS,)), dma((3 * CHUNKS,)),
-        dma((3 * CHUNKS,)), dma((3 * CHUNKS,)),
-        dma((3 * CHUNKS,)), dma((3 * CHUNKS,)),
-        dma((21,)), dma((21,)),
+        dma((7,)), dma((7,)),
     ]
     outs = pl.pallas_call(
         kernel,
-        out_shape=(block, block, block, block, jax.ShapeDtypeStruct(encodings.shape, BF16)),
+        out_shape=(
+            jax.ShapeDtypeStruct((3,) + self_query.shape[1:], BF16), block,
+            jax.ShapeDtypeStruct(encodings.shape, BF16),
+        ),
         in_specs=in_specs,
-        out_specs=(any_space,) * 5,
+        out_specs=(any_space,) * 3,
         scratch_shapes=scratch,
         compiler_params=pltpu.CompilerParams(
             collective_id=0, has_side_effects=True, vmem_limit_bytes=32 * 2**20
@@ -527,7 +530,7 @@
     return pl.pallas_call(
         place_outputs,
         out_shape=(block, block, block, block, jax.ShapeDtypeStruct(encodings.shape, BF16)),
-        in_specs=[any_space] * 5,
+        in_specs=[any_space] * 3,
         out_specs=(pl.BlockSpec(memory_space=pltpu.HBM),) * 5,
         scratch_shapes=[dma((4 + POOL_DEV,))],
         name="place_outputs",

time: 61.1 us -> 60.5 us (level)
  no operation moved by 1% of the time
where the time goes in v3:
time: 60.5 us; the launch traced here: 60.4 us
  Pallas kernels  59.7 us (99%)
  between operations  0.64 us (1%)
    pallas_call x1, Pallas kernels, on_device(): pl.pallas_call(kernel, out_shape=(jax.ShapeDtypeStruct((3,) + self_query....  58.3 us
    pallas_call x1, Pallas kernels, on_device(): pl.pallas_call(place_outputs, out_shape=(block, block, block, block, jax....  1.41 us

profile of v3, /device:TPU:0, one launch (start us, length us, event | category | flops | bytes accessed | tf_op | source)
XLA Modules:
  0.0 60.4 jit_solution(14338400487784120829)
XLA Ops:
  0.6 58.3 %retro_backward.1 = (bf16[3,128,1024]{2,1,0:T(8,128)(2,1)S(1)}, bf16[1,128,1024]{2,1,0:T(8,128)(2,1)S(1)}, bf16[8,128,512]{2,1,0:T(8,128)(2,1)S(1)}) custom-call(bf16[1,128,1024]{2,1,0:T(8,128)(2,1)} %sq.1, bf16[1,128,1024]{2,1,0:T(8,128)(2,1)} %sk.1, bf16[1,128,1024]{2,1,0:T(8,128)(2,1)} %sv.1, bf16[1,128,1024]{2,1,0:T(8,128)(2,1)} %sg.1, s32[1,128]{1,0:T(1,128)} %docs.1, ...), custom_call_target="tpu_custom_call" | custom-call | tf_op jit(solution)/shard_map/retro_backward/pallas_call | solution.py:510
  59.0 1.4 %place_outputs.1 = (bf16[1,128,1024]{2,1,0:T(8,128)(2,1)}, bf16[1,128,1024]{2,1,0:T(8,128)(2,1)}, bf16[1,128,1024]{2,1,0:T(8,128)(2,1)}, bf16[1,128,1024]{2,1,0:T(8,128)(2,1)}, bf16[8,128,512]{2,1,0:T(8,128)(2,1)}) custom-call(bf16[3,128,1024]{2,1,0:T(8,128)(2,1)S(1)} %get-tuple-element.8.own, bf16[1,128,1024]{2,1,0:T(8,128)(2,1)S(1)} %get-tuple-element.9.cross, ...), custom_call_target="tpu_custom_call" | custom-call | tf_op jit(solution)/shard_map/place_outputs/pallas_call | solution.py:530

commit v4 on v3

--- a/solution.py
+++ b/solution.py
@@ -25,9 +25,10 @@
 TILE = 256
 DOC_ROWS = 16
 QUARTER = E // N_HEAD
-CHUNKS = 4
+FETCH = ((0, 64), (64, 32), (96, 32))
+BACK = ((0, 32), (32, 32), (64, 64))
 ORDER_BACK = (4, 5, 7, 6, 1, 3, 2)
-CHUNK = NR // CHUNKS
+CHUNKS = len(FETCH)
 
 MESH = pl.DeviceIdType.MESH
 F32 = jnp.float32
@@ -113,7 +114,7 @@
     pl.semaphore_wait(barrier, len(peers))
 
     def quarter_of(owner_column, t):
-        return enc.at[:, pl.ds(t * CHUNK, CHUNK), pl.ds(pl.multiple_of(owner_column * QUARTER, 128), QUARTER)]
+        return enc.at[:, pl.ds(*FETCH[t]), pl.ds(pl.multiple_of(owner_column * QUARTER, 128), QUARTER)]
 
     pool_copies = []
     pool_own = []
@@ -150,7 +151,7 @@
 
     for copy in staging:
         copy.wait()
-    self_start((1, 3, 2))
+    self_start((4, 6, 1, 3, 2))
     self_own.append(keep(staged.at[:, head_columns(c)], held.at[c]))
     cross_own = [keep(wk, wk_v), keep(wv, wv_v), keep(cq.at[0], cq_v), keep(cg.at[0], cg_v)]
 
@@ -167,7 +168,7 @@
     my_columns = pl.ds(pl.multiple_of(h * QUARTER, 128), QUARTER)
 
     def hand_out(t):
-        here = pl.ds(t * CHUNK, CHUNK)
+        here = pl.ds(*FETCH[t])
         pool_own[t].wait()
         for copy in pool_copies[t]:
             copy.wait_recv()
@@ -185,7 +186,7 @@
         incoming[t][pl.ds(r * ENTRIES, ENTRIES)] = outgoing[pl.ds(r * ENTRIES, ENTRIES), here]
 
     def spread(t):
-        here = pl.ds(t * CHUNK, CHUNK)
+        here = pl.ds(*FETCH[t])
         for copy in ret_copies[t]:
             copy.wait_recv()
         for e in range(ENTRIES):
@@ -202,7 +203,7 @@
         if t < CHUNKS:
             hand_out(t)
         if t == CHUNKS - 1:
-            self_start((4, 5, 7, 6))
+            self_start((5, 7))
         if t >= 1:
             spread(t - 1)
 
@@ -298,22 +299,23 @@
         return [slice(n * width, (n + 1) * width) for n in range(keys_b.shape[2] // width)]
 
     def project(t):
-        here = slice(t * CHUNK, (t + 1) * CHUNK)
+        first, size = FETCH[t]
+        here = slice(first, first + size)
         for copy in row_copies[t]:
             copy.wait_recv()
-        tokens = rows[:, here, :].reshape(ENTRIES * CHUNK, E)
+        tokens = rows[:, here, :].reshape(ENTRIES * size, E)
         for cols in pieces(TILE):
             keys_raw = dot(tokens, wk_v[:, cols])
-            values_b[:, here, cols] = dot(tokens, wv_v[:, cols]).astype(BF16).reshape(ENTRIES, CHUNK, TILE)
+            values_b[:, here, cols] = dot(tokens, wv_v[:, cols]).astype(BF16).reshape(ENTRIES, size, TILE)
             for a in range(2):
                 one = keys_raw[:, a * DH:(a + 1) * DH]
                 mean = jnp.sum(one * one, axis=1, keepdims=True) * (1.0 / DH)
                 factor = jnp.broadcast_to(lax.rsqrt(mean + EPSILON), one.shape)
                 normed = one * factor
                 at = slice(cols.start + a * DH, cols.start + (a + 1) * DH)
-                factors[:, here, at] = factor.reshape(ENTRIES, CHUNK, DH)
-                keys_n[:, here, at] = normed.reshape(ENTRIES, CHUNK, DH)
-                keys_b[:, here, at] = normed.astype(BF16).reshape(ENTRIES, CHUNK, DH)
+                factors[:, here, at] = factor.reshape(ENTRIES, size, DH)
+                keys_n[:, here, at] = normed.reshape(ENTRIES, size, DH)
+                keys_b[:, here, at] = normed.astype(BF16).reshape(ENTRIES, size, DH)
 
     for t in range(CHUNKS):
         project(t)
@@ -363,13 +365,14 @@
     cross_done = keep(cross_out, ocq.at[0])
 
     def scatter(t):
-        here = pl.ds(t * CHUNK, CHUNK)
-        shape = (ENTRIES * CHUNK, keys_b.shape[2])
+        first, size = BACK[t]
+        here = pl.ds(first, size)
+        shape = (ENTRIES * size, keys_b.shape[2])
         term = dot_nt(raw_grads[:, here, :].reshape(shape), wk_v[...])
         term = term + dot_nt(value_grads[:, here, :].reshape(shape), wv_v[...])
         for q in range(N_HEAD):
             one = term[:, q * QUARTER:(q + 1) * QUARTER].astype(BF16)
-            parts_out[q, :, here, :] = one.reshape(ENTRIES, CHUNK, QUARTER)
+            parts_out[q, :, here, :] = one.reshape(ENTRIES, size, QUARTER)
         return [
             send(
                 parts_out.at[over_head(d), :, here], parts_in.at[h, :, here],
@@ -381,7 +384,8 @@
     part_copies = [scatter(t) for t in range(CHUNKS)]
 
     def share(t):
-        here = pl.ds(t * CHUNK, CHUNK)
+        first, size = BACK[t]
+        here = pl.ds(first, size)
         for copy in part_copies[t]:
             copy.wait_recv()
         total = parts_out[h, :, here, :].astype(F32)
@@ -403,12 +407,14 @@
     def hand_back(t):
         for copy in share_copies[t]:
             copy.wait_recv()
-        for k in range(CHUNK // GROUP):
-            at = slice(t * CHUNK + k * GROUP, t * CHUNK + (k + 1) * GROUP)
+        first, size = BACK[t]
+        for k in range(size // GROUP):
+            at = slice(first + k * GROUP, first + (k + 1) * GROUP)
             stacked = shares[:, at].reshape(N_RET * ENTRIES * GROUP, QUARTER)
             summed = dot(selector[...], stacked)
             owned[:, at] = summed.astype(BF16).reshape(N_HEAD * POOL_DEV, GROUP, QUARTER)
-        here = pl.ds(t * CHUNK, CHUNK)
+        first, size = BACK[t]
+        here = pl.ds(first, size)
         for d in (1, 3, 2):
             own_copies.append(send(
                 owned.at[pl.ds(over_head(d) * POOL_DEV, POOL_DEV), here], oenc.at[:, here, my_columns],
@@ -423,18 +429,15 @@
     self_rows(0)
     self_rows(1)
     share_copies.append(share(0))
+    self_rows(2)
     share_copies.append(share(1))
-    self_rows(2)
-    share_copies.append(share(2))
-    share_copies.append(share(3))
-    hand_back(0)
-    flush(3 + 3 * CHUNKS)
     self_rows(3)
     self_finish()
+    share_copies.append(share(2))
+    back_copies, back_own = self_back()
+    hand_back(0)
     hand_back(1)
-    back_copies, back_own = self_back()
     hand_back(2)
-    hand_back(3)
 
     cross_done.wait()
     for copy in back_own + own_kept:
@@ -472,9 +475,9 @@
         pltpu.VMEM((1, BLOCK), jnp.int32),
         pltpu.VMEM((N_CTX * BLOCK, 128), F32),
         pltpu.VMEM((4 * BLOCK + DOC_ROWS, N_CTX * DH), BF16),
-        (pltpu.VMEM((N_HEAD * POOL_DEV, CHUNK, QUARTER), BF16),) * CHUNKS,
+        tuple(pltpu.VMEM((N_HEAD * POOL_DEV, size, QUARTER), BF16) for _, size in FETCH),
         pltpu.VMEM((N_RET * ENTRIES, NR, QUARTER), BF16),
-        (pltpu.VMEM((N_RET * ENTRIES, CHUNK, QUARTER), BF16),) * CHUNKS,
+        tuple(pltpu.VMEM((N_RET * ENTRIES, size, QUARTER), BF16) for _, size in FETCH),
         pltpu.VMEM((ENTRIES, NR, E), BF16),
         pltpu.VMEM((N_CTX, 4 * BLOCK + DOC_ROWS, DH), BF16),
         pltpu.VMEM((N_CTX * BLOCK, DH), F32),

time: 60.5 us -> 58.2 us (0.962)
  Pallas kernels: 59.7 us -> 57.4 us
    pallas_call x1, Pallas kernels: 58.3 us -> 56 us  [on_device(): pl.pallas_call(kernel, out_shape=(jax.ShapeDtypeStruct((3,) + self_query....]
where the time goes in v4:
time: 58.2 us; the launch traced here: 58.1 us
  Pallas kernels  57.4 us (99%)
  between operations  0.64 us (1%)
    pallas_call x1, Pallas kernels, on_device(): pl.pallas_call(kernel, out_shape=(jax.ShapeDtypeStruct((3,) + self_query....  56 us
    pallas_call x1, Pallas kernels, on_device(): pl.pallas_call(place_outputs, out_shape=(block, block, block, block, jax....  1.41 us

profile of v4, /device:TPU:0, one launch (start us, length us, event | category | flops | bytes accessed | tf_op | source)
XLA Modules:
  0.0 58.1 jit_solution(4099708460505264978)
XLA Ops:
  0.6 56.0 %retro_backward.1 = (bf16[3,128,1024]{2,1,0:T(8,128)(2,1)S(1)}, bf16[1,128,1024]{2,1,0:T(8,128)(2,1)S(1)}, bf16[8,128,512]{2,1,0:T(8,128)(2,1)S(1)}) custom-call(bf16[1,128,1024]{2,1,0:T(8,128)(2,1)} %sq.1, bf16[1,128,1024]{2,1,0:T(8,128)(2,1)} %sk.1, bf16[1,128,1024]{2,1,0:T(8,128)(2,1)} %sv.1, bf16[1,128,1024]{2,1,0:T(8,128)(2,1)} %sg.1, s32[1,128]{1,0:T(1,128)} %docs.1, ...), custom_call_target="tpu_custom_call" | custom-call | tf_op jit(solution)/shard_map/retro_backward/pallas_call | solution.py:513
  56.7 1.4 %place_outputs.1 = (bf16[1,128,1024]{2,1,0:T(8,128)(2,1)}, bf16[1,128,1024]{2,1,0:T(8,128)(2,1)}, bf16[1,128,1024]{2,1,0:T(8,128)(2,1)}, bf16[1,128,1024]{2,1,0:T(8,128)(2,1)}, bf16[8,128,512]{2,1,0:T(8,128)(2,1)}) custom-call(bf16[3,128,1024]{2,1,0:T(8,128)(2,1)S(1)} %get-tuple-element.8.own, bf16[1,128,1024]{2,1,0:T(8,128)(2,1)S(1)} %get-tuple-element.9.cross, ...), custom_call_target="tpu_custom_call" | custom-call | tf_op jit(solution)/shard_map/place_outputs/pallas_call | solution.py:533

commit v5 on v4

--- a/solution.py
+++ b/solution.py
@@ -27,7 +27,7 @@
 QUARTER = E // N_HEAD
 FETCH = ((0, 64), (64, 32), (96, 32))
 BACK = ((0, 32), (32, 32), (64, 64))
-ORDER_BACK = (4, 5, 7, 6, 1, 3, 2)
+ORDER_BACK = (6, 5, 7, 4, 2, 1, 3)
 CHUNKS = len(FETCH)
 
 MESH = pl.DeviceIdType.MESH
@@ -434,8 +434,8 @@
     self_rows(3)
     self_finish()
     share_copies.append(share(2))
+    hand_back(0)
     back_copies, back_own = self_back()
-    hand_back(0)
     hand_back(1)
     hand_back(2)
 

time: 58.2 us -> 57.7 us (level)
  no operation moved by 1% of the time
where the time goes in v5:
time: 57.7 us; the launch traced here: 57.6 us
  Pallas kernels  56.9 us (99%)
  between operations  0.64 us (1%)
    pallas_call x1, Pallas kernels, on_device(): pl.pallas_call(kernel, out_shape=(jax.ShapeDtypeStruct((3,) + self_query....  55.5 us
    pallas_call x1, Pallas kernels, on_device(): pl.pallas_call(place_outputs, out_shape=(block, block, block, block, jax....  1.41 us

profile of v5, /device:TPU:0, one launch (start us, length us, event | category | flops | bytes accessed | tf_op | source)
XLA Modules:
  0.0 57.6 jit_solution(15960102898463523579)
XLA Ops:
  0.6 55.5 %retro_backward.1 = (bf16[3,128,1024]{2,1,0:T(8,128)(2,1)S(1)}, bf16[1,128,1024]{2,1,0:T(8,128)(2,1)S(1)}, bf16[8,128,512]{2,1,0:T(8,128)(2,1)S(1)}) custom-call(bf16[1,128,1024]{2,1,0:T(8,128)(2,1)} %sq.1, bf16[1,128,1024]{2,1,0:T(8,128)(2,1)} %sk.1, bf16[1,128,1024]{2,1,0:T(8,128)(2,1)} %sv.1, bf16[1,128,1024]{2,1,0:T(8,128)(2,1)} %sg.1, s32[1,128]{1,0:T(1,128)} %docs.1, ...), custom_call_target="tpu_custom_call" | custom-call | tf_op jit(solution)/shard_map/retro_backward/pallas_call | solution.py:513
  56.2 1.4 %place_outputs.1 = (bf16[1,128,1024]{2,1,0:T(8,128)(2,1)}, bf16[1,128,1024]{2,1,0:T(8,128)(2,1)}, bf16[1,128,1024]{2,1,0:T(8,128)(2,1)}, bf16[1,128,1024]{2,1,0:T(8,128)(2,1)}, bf16[8,128,512]{2,1,0:T(8,128)(2,1)}) custom-call(bf16[3,128,1024]{2,1,0:T(8,128)(2,1)S(1)} %get-tuple-element.8.own, bf16[1,128,1024]{2,1,0:T(8,128)(2,1)S(1)} %get-tuple-element.9.cross, ...), custom_call_target="tpu_custom_call" | custom-call | tf_op jit(solution)/shard_map/place_outputs/pallas_call | solution.py:533
